TPU v7x, 128 devices: a whole 4x4x4 slice. The times are simulated.
128 devices in a mesh: fsdp: 4 (over y), tok: 32 (over x, z, core).
Axes of the slice: x: 4, y: 4, z: 4, core: 2. Of those that a mesh axis runs over, the one named last changes fastest.
Arguments:
- tokens: bfloat16 [32768, 8192], P(('fsdp', 'tok')), may hold values from -6 to 6
- frozen_value_weight: bfloat16 [8192, 1024], P(None, 'fsdp'), may hold values from -0.0625 to 0.0625
- adapter_down_maps: bfloat16 [8192, 4096], P('tok', 'fsdp'), may hold values from -0.0625 to 0.0625
- adapter_up_maps: bfloat16 [1024, 4096], P('tok', 'fsdp'), may hold values from -1.5 to 1.5
- cotangent: bfloat16 [32768, 1024], P(('fsdp', 'tok')), may hold values from -6 to 6
- packing_block_tenant: int32 [256], replicated, may hold values from 0 to 255
- packing_block_fill: int32 [256], replicated, may hold values from 1 to 128
Outputs:
- values: bfloat16 [32768, 1024], P(('fsdp', 'tok'))
- token_gradient: bfloat16 [32768, 8192], P(('fsdp', 'tok'))
- grad_down: float32 [8192, 4096], P('tok', 'fsdp')
- grad_up: float32 [1024, 4096], P('tok', 'fsdp')
All inputs are finite; a program needn't handle non-finite values.
Results may differ from a plain program's by a relative error of at most 0.0055.
Values may be sent and summed in bfloat16 or wider, within the bound.
A program may use at most 128 MiB of HBM per device.

v0:
```python
import jax
import jax.numpy as jnp
from jax import lax
from jax.sharding import PartitionSpec as P

ADAPTER_RANK = 16
TENANT_COUNT = 256
BLOCK = 128


ADAPTER_SCALE = 2.0


def pick_columns(panel, tenants):
    grouped = panel.reshape(panel.shape[0], TENANT_COUNT, ADAPTER_RANK)
    return jnp.take(grouped, tenants, axis=1)


def local(
    tokens,
    frozen_value_weight,
    adapter_down_maps,
    adapter_up_maps,
    cotangent,
    packing_block_tenant,
    packing_block_fill,
):
    tok_rows = tokens.shape[0]
    dev_blocks = tok_rows // BLOCK
    tok_count = lax.axis_size("tok")
    group_blocks = dev_blocks * tok_count
    tenant_group_rows = group_blocks * BLOCK
    fsdp_here = lax.axis_index("fsdp")
    tok_here = lax.axis_index("tok")
    first_block = (fsdp_here * tok_count + tok_here) * dev_blocks
    my_fill = lax.dynamic_slice_in_dim(packing_block_fill, first_block, dev_blocks)
    used_rows = (jnp.arange(BLOCK, dtype=jnp.int32)[None, :] < my_fill[:, None]).reshape(
        tok_rows, 1
    )
    masked_token_rows = used_rows.astype(jnp.float32)
    grad_out = cotangent * used_rows.astype(jnp.bfloat16)
    group_tenants = lax.dynamic_slice_in_dim(
        packing_block_tenant, fsdp_here * group_blocks, group_blocks
    )
    one_hot = (group_tenants[:, None] == jnp.arange(TENANT_COUNT, dtype=jnp.int32)[None, :]).astype(
        jnp.float32
    )
    weight_full, down_full, up_full = (
        lax.all_gather(frozen_value_weight, "fsdp", axis=1, tiled=True),
        lax.all_gather(adapter_down_maps, "fsdp", axis=1, tiled=True),
        lax.all_gather(adapter_up_maps, "fsdp", axis=1, tiled=True),
    )
    frozen_output = jnp.dot(tokens, weight_full, preferred_element_type=jnp.float32)
    feat_cols, grad_cols = (
        lax.all_to_all(tokens, "tok", split_axis=1, concat_axis=0, tiled=True),
        lax.all_to_all(grad_out, "tok", split_axis=1, concat_axis=0, tiled=True),
    )
    feature_blocks = feat_cols.reshape(group_blocks, BLOCK, feat_cols.shape[1])
    gradient_blocks = grad_cols.reshape(group_blocks, BLOCK, grad_cols.shape[1])
    selected_down_map = pick_columns(down_full, group_tenants)
    up_sel = pick_columns(up_full, group_tenants)
    rank_part = jnp.einsum(
        "vxi,ivf->fvx", feature_blocks, selected_down_map, preferred_element_type=jnp.float32
    )
    back_part = jnp.einsum(
        "bkc,cbr->rbk", gradient_blocks, up_sel, preferred_element_type=jnp.float32
    )
    rank_total, back_total = lax.psum((rank_part, back_part), "tok")
    rank_space_input = rank_total.astype(jnp.bfloat16)
    rank_space_gradient = (ADAPTER_SCALE * back_total).astype(jnp.bfloat16)
    adapter_column_slice = (
        ADAPTER_SCALE
        * jnp.einsum("rbk,cbr->bkc", rank_space_input, up_sel, preferred_element_type=jnp.float32)
    ).astype(jnp.bfloat16)
    back_cols = jnp.einsum(
        "new,ien->ewi", rank_space_gradient, selected_down_map, preferred_element_type=jnp.float32
    ).astype(jnp.bfloat16)
    adapter_token_rows, backward_token_rows = (
        lax.all_to_all(
            adapter_column_slice.reshape(tenant_group_rows, -1),
            "tok",
            split_axis=0,
            concat_axis=1,
            tiled=True,
        ),
        lax.all_to_all(
            back_cols.reshape(tenant_group_rows, -1), "tok", split_axis=0, concat_axis=1, tiled=True
        ),
    )
    down_terms = jnp.einsum(
        "oum,eou->oem", feature_blocks, rank_space_gradient, preferred_element_type=jnp.float32
    )
    up_terms = ADAPTER_SCALE * jnp.einsum(
        "bkc,rbk->brc", gradient_blocks, rank_space_input, preferred_element_type=jnp.float32
    )
    down_part = jnp.einsum(
        "bg,brd->dgr", one_hot, down_terms, precision=lax.Precision.HIGHEST
    ).reshape(down_terms.shape[2], TENANT_COUNT * ADAPTER_RANK)
    up_part = jnp.einsum("bg,brc->cgr", one_hot, up_terms, precision=lax.Precision.HIGHEST).reshape(
        up_terms.shape[2], TENANT_COUNT * ADAPTER_RANK
    )
    down_sum, up_sum = (
        lax.psum_scatter(down_part, "fsdp", scatter_dimension=1, tiled=True),
        lax.psum_scatter(up_part, "fsdp", scatter_dimension=1, tiled=True),
    )
    values = (masked_token_rows * (frozen_output + adapter_token_rows.astype(jnp.float32))).astype(
        jnp.bfloat16
    )
    frozen_backward = lax.dot_general(
        grad_out, weight_full, (((1,), (1,)), ((), ())), preferred_element_type=jnp.float32
    )
    token_gradient = (frozen_backward + backward_token_rows.astype(jnp.float32)).astype(
        jnp.bfloat16
    )
    tenant_match = (
        packing_block_tenant[:, None] == jnp.arange(TENANT_COUNT, dtype=jnp.int32)[None, :]
    )
    counts = jnp.sum(
        jnp.where(tenant_match, packing_block_fill[:, None].astype(jnp.float32), 0.0), axis=0
    )
    denominator = jnp.repeat(jnp.maximum(counts, 1.0), ADAPTER_RANK)
    cols_here = down_sum.shape[1]
    denom_here = lax.dynamic_slice_in_dim(denominator, fsdp_here * cols_here, cols_here)
    return (values, token_gradient, down_sum / denom_here, up_sum / denom_here)


def solution(mesh):
    placed = (
        P(("fsdp", "tok"), None),
        P(None, "fsdp"),
        P("tok", "fsdp"),
        P("tok", "fsdp"),
        P(("fsdp", "tok"), None),
        P(),
        P(),
    )
    return jax.shard_map(
        local,
        mesh=mesh,
        in_specs=placed,
        out_specs=(
            P(("fsdp", "tok"), None),
            P(("fsdp", "tok"), None),
            P("tok", "fsdp"),
            P("tok", "fsdp"),
        ),
        check_vma=False,
    )
```

profile of v0, /device:TPU:1, one launch (start us, length us, event | category | flops | bytes accessed | tf_op | source)
XLA Modules:
  0.0 488.8 jit_solution(8441843618039830346)
XLA Ops:
  8.0 0.8 dynamic_slice.9
  8.8 1.2 copy.50
  10.1 0.8 broadcast_multiply_fusion
  10.9 9.4 %all-to-all-start.2 = ((bf16[256,32,32]{0,2,1:T(8,128)(2,1)}), bf16[256,32,32]{0,2,1:T(8,128)(2,1)S(1)}, u32[]{:S(2)}, u32[]{:S(2)}) async-start(bf16[256,32,32]{0,2,1:T(8,128)(2,1)} %bitcast.11), calls=%async_computation.2 | async-start | bytes 1048576 | tf_op jit(solution)/shard_map/all_to_all | solution.py:56
  20.4 4.7 copy.72
  25.1 6.9 %all-to-all-done.2 = bf16[256,32,32]{0,2,1:T(8,128)(2,1)S(1)} async-done(((bf16[256,32,32]{0,2,1:T(8,128)(2,1)}), bf16[256,32,32]{0,2,1:T(8,128)(2,1)S(1)}, u32[]{:S(2)}, u32[]{:S(2)}) %all-to-all-start.2) | async-done | bytes 524320 | tf_op jit(solution)/shard_map/all_to_all | solution.py:56
  32.0 4.8 all-to-all-start
  36.8 1.0 copy.44
  37.9 11.1 %all_gather.11 = bf16[32,4096]{1,0:T(8,128)(2,1)S(1)} all-gather(bf16[32,1024]{1,0:T(8,128)(2,1)S(1)} %copy-done.3), channel_id=1, replica_groups=mesh['fsdp'=4,'tok'=32] {'fsdp'}, dimensions={1}, use_global_device_ids=true | all-gather | bytes 327680 | tf_op jit(solution)/shard_map/all_gather | solution.py:51
  49.0 0.5 copy.46
  49.6 0.6 gather_fusion.1
  50.2 0.3 copy.51
  50.5 0.2 reshape.96
  50.7 1.3 convolution_bitcast_fusion.2
  52.0 19.6 %all-gather.5.cloned.1.call-done = bf16[256,4096]{0,1:T(8,128)(2,1)} async-done(((bf16[256,1024]{0,1:T(8,128)(2,1)}), bf16[256,4096]{0,1:T(8,128)(2,1)}) %all-gather.5.cloned.1.call-update) | async-done | bytes 2097168 | tf_op jit(solution)/shard_map/all_gather | solution.py:50
  71.6 2.2 gather_fusion
  73.8 15.6 %all-to-all-done = bf16[256,32,256]{2,0,1:T(8,128)(2,1)} async-done(((bf16[256,32,256]{2,0,1:T(8,128)(2,1)}), bf16[256,32,256]{2,0,1:T(8,128)(2,1)}, u32[]{:S(2)}, u32[]{:S(2)}) %all-to-all-start) | async-done | bytes 4194336 | tf_op jit(solution)/shard_map/all_to_all | solution.py:55
  89.4 3.4 convolution_bitcast_fusion.3
  92.8 123.9 %all-reduce.4 = bf16[16,64,128]{2,0,1:T(8,128)(2,1)S(1)} all-reduce(f32[16,64,128]{2,0,1:T(8,128)S(1)} %convolution_bitcast_fusion.3), channel_id=1, replica_groups=mesh['fsdp'=4,'tok'=32] {'tok'}, use_global_device_ids=true, to_apply=%region_0.1 | all-reduce | flops 131072 | bytes 786432 | tf_op jit(solution)/shard_map/psum | solution.py:68
  216.7 0.4 convolution_multiply_fusion.1
  217.2 0.6 convolution_bitcast_fusion.1
  217.8 2.5 copy.58
  220.4 3.0 fusion.14
  223.4 2.3 convolution_bitcast_fusion
  225.8 4.4 copy.55
  230.2 0.2 all-gather.3.cloned.1.call-start
  230.4 0.3 all-gather.3.cloned.1.call-update
  230.8 0.7 fusion.2
  231.4 0.2 copy.47
  231.6 0.2 all_to_all.47
  231.8 1.1 copy.48
  232.9 9.3 %all-to-all-start.1 = ((bf16[32,256,32]{1,2,0:T(8,128)(2,1)}), bf16[32,256,32]{1,2,0:T(8,128)(2,1)S(1)}, u32[]{:S(2)}, u32[]{:S(2)}) async-start(bf16[32,256,32]{1,2,0:T(8,128)(2,1)} %copy.48), calls=%async_computation.1 | async-start | bytes 1048576 | tf_op jit(solution)/shard_map/all_to_all | solution.py:79
  242.2 3.3 convolution_convert_fusion
  245.5 8.4 %all-to-all-done.1 = bf16[32,256,32]{1,2,0:T(8,128)(2,1)S(1)} async-done(((bf16[32,256,32]{1,2,0:T(8,128)(2,1)}), bf16[32,256,32]{1,2,0:T(8,128)(2,1)S(1)}, u32[]{:S(2)}, u32[]{:S(2)}) %all-to-all-start.1) | async-done | bytes 524320 | tf_op jit(solution)/shard_map/all_to_all | solution.py:79
  253.9 4.8 all-to-all-start.3
  258.7 0.1 select_reduce_fusion
  259.1 0.1 convert_element_type.81
  259.2 1.3 copy.49
  260.5 1.2 broadcast_divide_fusion.1
  261.8 0.8 copy.60
  262.6 48.0 %all-to-all-done.3 = bf16[32,256,256]{2,1,0:T(8,128)(2,1)} async-done(((bf16[32,256,256]{2,1,0:T(8,128)(2,1)}), bf16[32,256,256]{2,1,0:T(8,128)(2,1)}, u32[]{:S(2)}, u32[]{:S(2)}) %all-to-all-start.3) | async-done | bytes 4194336 | tf_op jit(solution)/shard_map/all_to_all | solution.py:86
  310.6 3.9 convert_bitcast_fusion
  314.5 4.6 copy.62
  319.1 1.4 broadcast_divide_fusion
  320.5 1.3 copy.59
  321.8 137.5 %all-gather.3.cloned.1.call-done = bf16[8192,1024]{1,0:T(8,128)(2,1)} async-done(((bf16[8192,256]{1,0:T(8,128)(2,1)}), bf16[8192,1024]{1,0:T(8,128)(2,1)}) %all-gather.3.cloned.1.call-update) | async-done | bytes 16777232 | tf_op jit(solution)/shard_map/all_gather | solution.py:49
  459.4 12.9 %fusion = bf16[256,8192]{1,0:T(8,128)(2,1)} fusion(f32[256,8192]{1,0:T(8,128)} %bitcast.59, bf16[256,1024]{0,1:T(8,128)(2,1)} %broadcast_multiply_fusion, bf16[8192,1024]{1,0:T(8,128)(2,1)} %all-gather.3.cloned.1.call-done), kind=kOutput, calls=%fused_computation.3 | convolution fusion | flops 4299161600 | bytes 29884416 | tf_op jit(solution)/shard_map/dot_general | solution.py:109
  472.3 9.4 %fusion.3 = bf16[256,1024]{1,0:T(8,128)(2,1)} fusion(f32[256,1024]{1,0:T(8,128)} %copy.49, bf16[256,8192]{1,0:T(8,128)(2,1)S(1)} %copy-done, bf16[8192,1024]{1,0:T(8,128)(2,1)} %all-gather.3.cloned.1.call-done, f32[256]{0:T(256)S(1)} %get-tuple-element.19), kind=kOutput, calls=%fused_computation.12 | convolution fusion | flops 4295753728 | bytes 22545408 | tf_op jit(solution)/shard_map/dot_general | solution.py:53
  (32 shorter events, 0.7 us)
Async XLA Ops:
  10.9 21.1 %all-to-all-start.2 = ((bf16[256,32,32]{0,2,1:T(8,128)(2,1)}), bf16[256,32,32]{0,2,1:T(8,128)(2,1)S(1)}, u32[]{:S(2)}, u32[]{:S(2)}) async-start(bf16[256,32,32]{0,2,1:T(8,128)(2,1)} %bitcast.11), calls=%async_computation.2 | async-start | bytes 1048576 | tf_op jit(solution)/shard_map/all_to_all | solution.py:56
  32.0 4.8 copy-start.2
  32.0 5.9 %copy-start.3 = (bf16[32,1024]{1,0:T(8,128)(2,1)S(1)}, bf16[32,1024]{1,0:T(8,128)(2,1)}, u32[]{:S(2)}) copy-start(bf16[32,1024]{1,0:T(8,128)(2,1)} %param.10) | copy-start | bytes 196612
  32.0 17.5 %copy-start.4 = (s32[256]{0:T(256)S(1)}, s32[256]{0:T(256)}, u32[]{:S(2)}) copy-start(s32[256]{0:T(256)} %param.12) | copy-start | bytes 3076
  32.0 57.4 %all-to-all-start = ((bf16[256,32,256]{2,0,1:T(8,128)(2,1)}), bf16[256,32,256]{2,0,1:T(8,128)(2,1)}, u32[]{:S(2)}, u32[]{:S(2)}) async-start(bf16[256,32,256]{2,0,1:T(8,128)(2,1)} %bitcast.61), calls=%async_computation | async-start | bytes 8388608 | tf_op jit(solution)/shard_map/all_to_all | solution.py:55
  36.8 34.8 %all-gather.5.cloned.1.call-start = ((), (), s32[]{:S(2)}) async-start(), calls=%async_computation.7 | async-start | bytes 2621440 | tf_op jit(solution)/shard_map/all_gather | solution.py:50
  37.8 182.5 %all-reduce.3.cloned.1.call-start = ((), (), s32[]{:S(2)}) async-start(), calls=%async_computation.8 | async-start | bytes 1048576 | tf_op jit(solution)/shard_map/psum | solution.py:68
  52.0 208.5 %reduce-scatter.5.cloned.1.call-start = ((), (), s32[]{:S(2)}) async-start(), calls=%async_computation.10 | async-start | bytes 2621440 | tf_op jit(solution)/shard_map/reduce_scatter | solution.py:104
  220.3 98.8 %reduce-scatter.3.cloned.1.call-start = ((), (), s32[]{:S(2)}) async-start(), calls=%async_computation.9 | async-start | bytes 5242880 | tf_op jit(solution)/shard_map/reduce_scatter | solution.py:103
  230.2 12.0 %copy-start.1 = (f32[16,64,128]{2,0,1:T(8,128)S(1)}, f32[16,64,128]{2,0,1:T(8,128)}, u32[]{:S(2)}) copy-start(f32[16,64,128]{2,0,1:T(8,128)} %all-reduce.3.cloned.1.call-done) | copy-start | bytes 1572868
  230.2 229.2 %all-gather.3.cloned.1.call-start = ((), (), s32[]{:S(2)}) async-start(), calls=%async_computation.6 | async-start | bytes 20971520 | tf_op jit(solution)/shard_map/all_gather | solution.py:49
  232.9 21.0 %all-to-all-start.1 = ((bf16[32,256,32]{1,2,0:T(8,128)(2,1)}), bf16[32,256,32]{1,2,0:T(8,128)(2,1)S(1)}, u32[]{:S(2)}, u32[]{:S(2)}) async-start(bf16[32,256,32]{1,2,0:T(8,128)(2,1)} %copy.48), calls=%async_computation.1 | async-start | bytes 1048576 | tf_op jit(solution)/shard_map/all_to_all | solution.py:79
  253.9 4.8 copy-start.5
  253.9 56.7 %all-to-all-start.3 = ((bf16[32,256,256]{2,1,0:T(8,128)(2,1)}), bf16[32,256,256]{2,1,0:T(8,128)(2,1)}, u32[]{:S(2)}, u32[]{:S(2)}) async-start(bf16[32,256,256]{2,1,0:T(8,128)(2,1)} %bitcast.62), calls=%async_computation.3 | async-start | bytes 8388608 | tf_op jit(solution)/shard_map/all_to_all | solution.py:86
  459.4 12.9 %copy-start = (bf16[256,8192]{1,0:T(8,128)(2,1)S(1)}, bf16[256,8192]{1,0:T(8,128)(2,1)}, u32[]{:S(2)}) copy-start(bf16[256,8192]{1,0:T(8,128)(2,1)} %param.7) | copy-start | bytes 12582916
Sparse Core Ops, SparseCore 0:
  39.8 31.7 all-gather.4
  220.4 31.2 reduce-scatter.4
  254.2 46.4 reduce-scatter.2
  302.3 157.0 all-gather.2
Sparse Core Ops, SparseCore 1:
  52.1 120.5 all-reduce.2
where the time goes:
time: 490 us; the launch traced here: 489 us
  waiting for transfers between devices  236 us (48%)
  blocking collectives  135 us (28%)
  matrix products  37.4 us (8%)
  starting transfers between devices  28.6 us (6%)
  local copies, waits for them, and re-layouts  28.1 us (6%)
  between operations  15.5 us (3%)
  other arithmetic  7.85 us (2%)
    all_gather x1, waiting for transfers between devices, local(): lax.all_gather(frozen_value_weight, 'fsdp', axis=1, tiled=True)  138 us
    psum x1, blocking collectives, local(): rank_total, back_total = lax.psum((rank_part, back_part), 'tok')  124 us
    all_to_all x1, waiting for transfers between devices, local(): lax.all_to_all(back_cols.reshape(tenant_group_rows, -1), 'tok', split_axi...  48 us
    all_gather x1, waiting for transfers between devices, local(): lax.all_gather(adapter_down_maps, 'fsdp', axis=1, tiled=True)  19.6 us
    all_to_all x1, waiting for transfers between devices, local(): lax.all_to_all(tokens, 'tok', split_axis=1, concat_axis=0, tiled=True)  15.6 us
    dot_general x1, matrix products, local(): lax.dot_general(grad_out, weight_full, (((1,), (1,)), ((), ())), preferre...  12.9 us
    all_gather x1, blocking collectives, local(): lax.all_gather(adapter_up_maps, 'fsdp', axis=1, tiled=True)  11.1 us
  transfers between devices with their start and end apart: 9, of which 6 were waited for; matrix products, arithmetic and copies ran while one was open for 10% of the time, Pallas kernels for 0%

commit v1 on v0

v1 whole, which is shorter than its diff:
```python
import jax
import jax.numpy as jnp
from jax import lax
from jax.experimental import pallas as pl
from jax.experimental.pallas import tpu as pltpu
from jax.sharding import PartitionSpec as P

RANK = 16
BLOCK = 128
SCALE = 2.0
BF = jnp.bfloat16
F32 = jnp.float32
NT = (((1,), (1,)), ((), ()))
TN = (((0,), (0,)), ((), ()))
PANEL = 1152
HALF = 576


def mm(a, b, dims=(((1,), (0,)), ((), ()))):
    return lax.dot_general(a, b, dims, preferred_element_type=F32)


def iota(shape, dim):
    return lax.broadcasted_iota(jnp.int32, shape, dim)


def pick(cond):
    return jnp.where(cond, 1.0, 0.0).astype(BF)


def kernel(
    x_hbm,
    w_hbm,
    panel,
    cot,
    tenant,
    fill,
    where,
    values,
    tgrad,
    gdown,
    gup,
    xv,
    wall,
    go,
    va,
    tga,
    aball,
    send_a,
    vb,
    send_b,
    at,
    recv_b,
    bt,
    gs,
    us,
    ur,
    terms,
    lo,
    rg_s,
    onehot,
    acc,
    cnt,
    loc,
    ab_sem,
    wy_sem,
    wx_sem,
    wc_sem,
    pa_sem,
    pb_sem,
    ga_sem,
    gu_sem,
    gy_sem,
):
    f = lax.axis_index("fsdp")
    t = lax.axis_index("tok")
    x = t // 8
    z = (t // 2) % 4
    c = t % 2

    def up(i, d):
        return lax.rem(i + d, 4)

    def dev_y(d):
        return (up(f, d), t)

    def dev_x(d):
        return (f, up(x, d) * 8 + z * 2 + c)

    def dev_z(d):
        return (f, x * 8 + up(z, d) * 2 + c)

    sibling = (f, x * 8 + z * 2 + (1 - c))

    def remote(src, dst, sem, i, dev):
        return pltpu.make_async_remote_copy(
            src_ref=src,
            dst_ref=dst,
            send_sem=sem.at[0, i],
            recv_sem=sem.at[1, i],
            device_id=dev,
            device_id_type=pl.DeviceIdType.MESH,
        )

    get_x = pltpu.make_async_copy(x_hbm, xv, loc.at[0])
    get_w = pltpu.make_async_copy(w_hbm, wall.at[f], loc.at[1])
    get_p = pltpu.make_async_copy(panel, aball.at[pl.ds(f * 72, 72)], loc.at[2])
    get_p.start()
    get_x.start()
    get_w.start()

    pending = []

    def ring_y(src_of, part_of, sem):
        first = {}
        for i, (d, s) in enumerate(((1, 0), (3, 1), (1, 1), (3, 0))):
            cp = remote(src_of(s), part_of(f, s), sem, i, dev_y(d))
            cp.start()
            first[d, s] = cp
            pending.append(cp)

        def forward():
            out = []
            for i, (d, s) in enumerate(((1, 0), (3, 1))):
                first[d, s].wait_recv()
                src = up(f, 4 - d)
                cp = remote(part_of(src, s), part_of(src, s), sem, 4 + i, dev_y(d))
                cp.start()
                out.append(cp)
                pending.append(cp)
            first[1, 1].wait_recv()
            first[3, 0].wait_recv()
            return out

        return forward

    ab_forward = ring_y(
        lambda s: panel.at[pl.ds(s * 36, 36)],
        lambda i, s: aball.at[pl.ds(i * 72 + s * 36, 36)],
        ab_sem,
    )

    b0 = (f * 32 + t) * 2
    rows = iota((256, 1), 0)
    limit = jnp.where(rows < BLOCK, fill[b0], fill[b0 + 1] + BLOCK)
    used = rows < limit
    for j in range(4):
        go[j] = jnp.where(used, cot[:, j * 256 : (j + 1) * 256].astype(F32), 0.0).astype(BF)
    va[...] = jnp.zeros_like(va)
    get_x.wait()
    get_w.wait()

    def own_step(k, carry):
        cols = pl.ds(pl.multiple_of(k * 256, 256), 256)
        wk = wall[f, cols, :]
        va[f] += mm(xv[:, cols], wk)
        tga[:, cols] = mm(go[f], wk, NT)
        return carry

    lax.fori_loop(0, 32, own_step, 0)

    tlane = (iota((1, 1024), 1) >> 4) + f * 64

    def count_step(b, total):
        return total + jnp.where(tlane == tenant[b], fill[b].astype(F32), 0.0)

    cnt[...] = lax.fori_loop(0, 256, count_step, jnp.zeros((1, 1024), F32))

    ab_last = ab_forward()

    base = (x * 1024 + c * 512, 4096 + z * 1024 + c * 512)

    def wslice(fi, row0):
        return wall.at[fi, pl.ds(pl.multiple_of(row0, 256), 256), :]

    wy = {}
    n_y = 0
    for h in range(2):
        for d, s in ((1, 0), (3, 1), (1, 1), (3, 0)):
            r0 = base[h] + s * 256
            cp = remote(
                w_hbm.at[pl.ds(pl.multiple_of(r0, 256), 256), :],
                wslice(f, r0),
                wy_sem,
                n_y,
                dev_y(d),
            )
            cp.start()
            wy[h, d, s] = cp
            pending.append(cp)
            n_y += 1

    for cp in ab_last:
        cp.wait_recv()
    get_p.wait()

    lane32 = iota((16, 256), 1) >> 5

    def pick_step(b, carry):
        dst = pl.ds(pl.multiple_of(b * 16, 16), 16)
        send_a[dst, :] = aball[where[0, f * 64 + b]]
        v = aball[where[1, f * 64 + b]]
        vb[dst, :] = jnp.where(lane32 == where[2, f * 64 + b], v.astype(F32), 0.0).astype(BF)
        return carry

    lax.fori_loop(0, 64, pick_step, 0)
    el = iota((256, 128), 0)
    ej = iota((256, 128), 1)
    spread = pick(((el & 31) == (ej & 31)) & ((ej >> 5) == (t & 3)))
    send_b[...] = mm(vb[...], spread).astype(BF)

    def my_cols(i, n):
        return pl.ds(pl.multiple_of(i * n, n), n)

    def swap_a(d):
        to = lax.rem(t + d, 32)
        return (
            remote(send_a.at[my_cols(to, 32), :], at.at[:, my_cols(t, 256)], pa_sem, d, (f, to)),
            remote(send_b.at[my_cols(to, 32), :], recv_b.at[t], pb_sem, d, (f, to)),
        )

    def swap_start(d, carry):
        for cp in swap_a(d):
            cp.start()
        return carry

    def swap_recv(d, carry):
        for cp in swap_a(d):
            cp.wait_recv()
        return carry

    def swap_sent(d, carry):
        for cp in swap_a(d):
            cp.wait_send()
        return carry

    lax.fori_loop(1, 32, swap_start, 0)
    at[:, my_cols(t, 256)] = send_a[my_cols(t, 32), :]
    recv_b[t] = send_b[my_cols(t, 32), :]

    wx = {}
    counters = {"x": 0, "c": 0}
    wc = {}
    foreign = (up(f, 3), up(f, 1), up(f, 2))

    def to_sibling(fi, r0, key):
        cp = remote(wslice(fi, r0), wslice(fi, r0), wc_sem, counters["c"], sibling)
        counters["c"] += 1
        cp.start()
        wc[key] = cp
        pending.append(cp)

    def to_plane(fi, r0, d, key, h):
        cp = remote(
            wslice(fi, r0), wslice(fi, r0), wx_sem, counters["x"], (dev_x if h == 0 else dev_z)(d)
        )
        counters["x"] += 1
        cp.start()
        wx[key] = cp
        pending.append(cp)

    fw = {}
    for h in range(2):
        for d, s in ((1, 0), (3, 1)):
            wy[h, d, s].wait_recv()
            src = up(f, 4 - d)
            r0 = base[h] + s * 256
            cp = remote(wslice(src, r0), wslice(src, r0), wy_sem, n_y, dev_y(d))
            n_y += 1
            cp.start()
            fw[h, s] = cp
            pending.append(cp)
        for d, s in ((1, 0), (3, 1), (1, 1), (3, 0)):
            if (d, s) in ((1, 1), (3, 0)):
                wy[h, d, s].wait_recv()
            fi = 0 if d == 1 else 1
            r0 = base[h] + s * 256
            for dd in (1, 3) if s == 0 else (3, 1):
                to_plane(foreign[fi], r0, dd, (h, dd, fi, s), h)
            to_sibling(foreign[fi], r0, (h, 0, fi, s))

    lax.fori_loop(1, 32, swap_recv, 0)
    for q in range(8):
        total = recv_b[4 * q]
        for i in range(1, 4):
            total = total + recv_b[4 * q + i]
        bt[:, q * 128 : (q + 1) * 128] = total

    def rank_step(k, total):
        cols = my_cols(k, 1024)
        return total + mm(xv[:, cols], at[:, cols], NT)

    diagonal = (iota((256, 32), 0) >> 7) == (iota((256, 32), 1) >> 4)
    rank_in = lax.fori_loop(0, 8, rank_step, jnp.zeros((256, 32), F32))
    rank_in = jnp.where(diagonal, rank_in, 0.0).astype(BF)
    rank_grad = jnp.zeros((256, 32), F32)
    for j in range(4):
        rank_grad = rank_grad + mm(go[j], bt[:, j * 256 : (j + 1) * 256], NT)
    rank_grad = jnp.where(diagonal, SCALE * rank_grad, 0.0).astype(BF)
    rg_s[...] = rank_grad

    def terms_step(k, carry):
        cols = my_cols(k, 1024)
        gs[:, cols] = mm(rg_s[...], xv[:, cols], TN).astype(BF)
        return carry

    lax.fori_loop(0, 8, terms_step, 0)
    for j in range(4):
        us[:, j * 256 : (j + 1) * 256] = (SCALE * mm(rank_in, go[j], TN)).astype(BF)

    def swap_g(d):
        to = lax.rem(t + d, 32)
        return (
            remote(gs.at[:, my_cols(to, 256)], terms.at[f, my_cols(t, 32), :], ga_sem, d, (f, to)),
            remote(us.at[:, my_cols(to // 4, 128)], ur.at[my_cols(t, 32), :], gu_sem, d, (f, to)),
        )

    def g_start(d, carry):
        for cp in swap_g(d):
            cp.start()
        return carry

    def g_recv(d, carry):
        for cp in swap_g(d):
            cp.wait_recv()
        return carry

    def g_sent(d, carry):
        for cp in swap_g(d):
            cp.wait_send()
        return carry

    lax.fori_loop(1, 32, g_start, 0)
    terms[f, my_cols(t, 32), :] = gs[:, my_cols(t, 256)]
    ur[my_cols(t, 32), :] = us[:, my_cols(t // 4, 128)]

    for j in range(4):
        lo[:, j * 256 : (j + 1) * 256] = (
            SCALE * mm(rank_in, bt[:, j * 256 : (j + 1) * 256])
        ).astype(BF)

    for h in range(2):
        for s in range(2):
            fw[h, s].wait_recv()
            r0 = base[h] + s * 256
            for dd in (1, 3) if s == 0 else (3, 1):
                to_plane(foreign[2], r0, dd, (h, dd, 2, s), h)
            to_sibling(foreign[2], r0, (h, 0, 2, s))

    lax.fori_loop(1, 32, g_recv, 0)
    packed = jnp.zeros((128, 256), F32)
    ul = iota((128, 256), 0)
    uj = iota((128, 256), 1)
    for q in range(8):
        e = pick(((ul >> 5) == (t & 3)) & ((uj >> 5) == q) & ((ul & 31) == (uj & 31)))
        packed = packed + mm(ur[q * 128 : (q + 1) * 128, :], e)
    terms[f, 1024:1152, :] = packed.astype(BF)
    g_forward = ring_y(
        lambda s: terms.at[f, pl.ds(s * HALF, HALF)],
        lambda i, s: terms.at[i, pl.ds(s * HALF, HALF)],
        gy_sem,
    )

    def here(h, d):
        if h == 0:
            return up(x, d) * 1024 + c * 512
        return 4096 + up(z, d) * 1024 + c * 512

    for fi in range(3):
        for h in range(2):
            for d, s in ((1, 0), (3, 1)):
                wx[h, d, fi, s].wait_recv()
                r0 = here(h, 4 - d) + s * 256
                to_plane(foreign[fi], r0, d, (h, 2, fi, s), h)
                to_sibling(foreign[fi], r0, (h, d, fi, s))
            for d, s in ((1, 1), (3, 0)):
                wx[h, d, fi, s].wait_recv()
                r0 = here(h, 4 - d) + s * 256
                to_sibling(foreign[fi], r0, (h, d, fi, s))

    def tile(row0):
        cols = pl.ds(pl.multiple_of(row0, 256), 256)
        xk = xv[:, cols]
        total = tga[:, cols] + mm(rg_s[...], at[:, cols])
        for fi in foreign:
            wk = wall[fi, cols, :]
            va[fi] += mm(xk, wk)
            total = total + mm(go[fi], wk, NT)
        tgrad[:, cols] = total.astype(BF)

    def tiles(d):
        def step(i, carry):
            h = i // 4
            pos = jnp.where(h == 0, lax.rem(x + d, 4), lax.rem(z + d, 4))
            tile(h * 4096 + pos * 1024 + (i % 4) * 256)
            return carry

        lax.fori_loop(0, 8, step, 0)

    def await_sibling(d):
        for h in range(2):
            for fi in range(3):
                for s in range(2):
                    wc[h, d, fi, s].wait_recv()

    await_sibling(0)
    tiles(0)

    g_last = g_forward()
    for d in (1, 3):
        await_sibling(d)
        tiles(4 - d)

    for fi in range(3):
        for h in range(2):
            for s in range(2):
                wx[h, 2, fi, s].wait_recv()
                to_sibling(foreign[fi], here(h, 2) + s * 256, (h, 2, fi, s))

    shift = iota((16, 1024), 1) - iota((16, 1024), 0) + f * 1024
    dl = iota((256, 128), 0)
    dj = iota((256, 128), 1)
    acc[...] = jnp.zeros_like(acc)

    def reduce_group(fi):
        def step(q, carry):
            for i in range(8):
                key = tenant[fi * 64 + q * 8 + i] * 16
                onehot[i * 16 : (i + 1) * 16, :] = pick(shift == key)
            unpack = pick((dl == q * 32 + dj) & (dj < 32))
            u = mm(terms[fi, 1024:1152, :], unpack).astype(BF)
            lhs = jnp.concatenate([terms[fi, my_cols(q, 128), :], u], axis=1)
            acc[...] += mm(lhs, onehot[...], TN)
            return carry

        lax.fori_loop(0, 8, step, 0)

    reduce_group(f)
    reduce_group(foreign[0])
    reduce_group(foreign[1])
    for cp in g_last:
        cp.wait_recv()
    reduce_group(foreign[2])
    denom = jnp.maximum(cnt[...], 1.0)
    gdown[...] = acc[0:256, :] / denom
    gup[...] = acc[256:288, :] / denom

    await_sibling(2)
    tiles(2)
    for j in range(4):
        cols = slice(j * 256, (j + 1) * 256)
        values[:, cols] = jnp.where(used, va[j] + lo[:, cols].astype(F32), 0.0).astype(BF)

    lax.fori_loop(1, 32, swap_sent, 0)
    lax.fori_loop(1, 32, g_sent, 0)
    for cp in pending:
        cp.wait_send()


def local(tokens, weight, down, up, cotangent, tenant, fill):
    side = up.reshape(32, 8, 8, 16).transpose(1, 3, 2, 0).reshape(128, 256)
    panel = jnp.concatenate([down.T, side], axis=0)
    owner, slot = tenant // 64, tenant % 64
    where = jnp.stack([owner * 72 + slot, owner * 72 + 64 + slot // 8, slot % 8])
    any_ = pl.BlockSpec(memory_space=pl.ANY)
    vmem = pl.BlockSpec(memory_space=pltpu.VMEM)
    smem = pl.BlockSpec(memory_space=pltpu.SMEM)
    dma = pltpu.SemaphoreType.DMA
    V = pltpu.VMEM
    return pl.pallas_call(
        kernel,
        out_shape=(
            jax.ShapeDtypeStruct((256, 1024), BF),
            jax.ShapeDtypeStruct((256, 8192), BF),
            jax.ShapeDtypeStruct((256, 1024), F32),
            jax.ShapeDtypeStruct((32, 1024), F32),
        ),
        in_specs=[any_, any_, vmem, vmem, smem, smem, smem],
        out_specs=(vmem, vmem, vmem, vmem),
        scratch_shapes=[
            V((256, 8192), BF),
            V((4, 8192, 256), BF),
            V((4, 256, 256), BF),
            V((4, 256, 256), F32),
            V((256, 8192), F32),
            V((288, 16, 256), BF),
            V((1024, 256), BF),
            V((1024, 256), BF),
            V((1024, 128), BF),
            V((32, 8192), BF),
            V((32, 32, 128), BF),
            V((32, 1024), BF),
            V((32, 8192), BF),
            V((32, 1024), BF),
            V((1024, 128), BF),
            V((4, PANEL, 256), BF),
            V((256, 1024), BF),
            V((256, 32), BF),
            V((128, 1024), BF),
            V((384, 1024), F32),
            V((1, 1024), F32),
            dma((3,)),
            dma((2, 6)),
            dma((2, 12)),
            dma((2, 36)),
            dma((2, 48)),
            dma((2, 32)),
            dma((2, 32)),
            dma((2, 32)),
            dma((2, 32)),
            dma((2, 6)),
        ],
        compiler_params=pltpu.CompilerParams(
            has_side_effects=True, vmem_limit_bytes=60 * 1024 * 1024
        ),
        cost_estimate=pl.CostEstimate(
            flops=9_000_000_000, bytes_accessed=30_000_000, transcendentals=0
        ),
    )(tokens, weight, panel.reshape(72, 16, 256), cotangent, tenant, fill, where)


def solution(mesh):
    placed = (
        P(("fsdp", "tok"), None),
        P(None, "fsdp"),
        P("tok", "fsdp"),
        P("tok", "fsdp"),
        P(("fsdp", "tok"), None),
        P(),
        P(),
    )
    return jax.shard_map(
        local,
        mesh=mesh,
        in_specs=placed,
        out_specs=(
            P(("fsdp", "tok"), None),
            P(("fsdp", "tok"), None),
            P("tok", "fsdp"),
            P("tok", "fsdp"),
        ),
        check_vma=False,
    )
```

time: 490 us -> 132 us (0.27)
  waiting for transfers between devices: 236 us -> 0 us
  blocking collectives: 135 us -> 0 us
  Pallas kernels: 0 us -> 118 us
  matrix products: 37.4 us -> 0 us
  starting transfers between devices: 28.6 us -> 0 us
  local copies, waits for them, and re-layouts: 28.1 us -> 10.7 us
  between operations: 15.5 us -> 0.67 us
  other arithmetic: 7.85 us -> 2.4 us
    all_gather x2 -> x0, waiting for transfers between devices: 157 us -> none  [the longest x1 138 us: local(): lax.all_gather(frozen_value_weight, 'fsdp', axis=1, tiled=True)]
    psum x1 -> x0, blocking collectives: 124 us -> none  [local(): rank_total, back_total = lax.psum((rank_part, back_part), 'tok')]
    pallas_call x0 -> x1, Pallas kernels: none -> 118 us  [local(): pl.pallas_call(kernel, out_shape=(jax.ShapeDtypeStruct((256, 1024), BF),...]
    all_to_all x4 -> x0, waiting for transfers between devices: 78.9 us -> none  [the longest x1 48 us: local(): lax.all_to_all(back_cols.reshape(tenant_group_rows, -1), 'tok', split_axi...]
    dot_general x10 -> x0, matrix products: 37.4 us -> none  [the longest x1 12.9 us: local(): lax.dot_general(grad_out, weight_full, (((1,), (1,)), ((), ())), preferre...]
    all_to_all x4 -> x0, starting transfers between devices: 28.2 us -> none  [the longest x1 9.43 us: local(): lax.all_to_all(grad_out, 'tok', split_axis=1, concat_axis=0, tiled=True)]
    all_gather x1 -> x0, blocking collectives: 11.1 us -> none  [local(): lax.all_gather(adapter_up_maps, 'fsdp', axis=1, tiled=True)]
    transpose x2 -> x1, local copies, waits for them, and re-layouts: 6.89 us -> 0.07 us  [local(): side = up.reshape(32, 8, 8, 16).transpose(1, 3, 2, 0).reshape(128, 256)]
  transfers between devices with their start and end apart: 9 -> 0, of which waited for: 6 -> 0; matrix products, arithmetic and copies ran while one was open for 10% -> 0% of each run, Pallas kernels for 0% -> 0%
where the time goes in v1:
time: 132 us
  Pallas kernels  118 us (89%)
  local copies, waits for them, and re-layouts  10.7 us (8%)
  other arithmetic  2.4 us (2%)
    pallas_call x1, Pallas kernels, local(): pl.pallas_call(kernel, out_shape=(jax.ShapeDtypeStruct((256, 1024), BF),...  118 us
    unnamed x9, local copies, waits for them, and re-layouts  9.24 us

profile of v1, /device:TPU:1, one launch (start us, length us, event | category | flops | bytes accessed | tf_op | source)
XLA Modules:
  0.0 131.9 jit_solution(4558548331507692116)
XLA Ops:
  0.6 0.7 fusion.2
  1.3 0.6 pad_add_fusion.where
  1.9 1.0 copy.13
  3.0 0.1 copy.14
  3.0 0.2 reshape.18
  3.2 0.1 copy.15
  3.3 1.1 pad_maximum_fusion
  4.4 1.1 copy.16
  5.5 118.2 %shard_map.102 = (bf16[256,1024]{1,0:T(8,128)(2,1)}, bf16[256,8192]{1,0:T(8,128)(2,1)}, f32[256,1024]{1,0:T(8,128)}, f32[32,1024]{1,0:T(8,128)}) custom-call(bf16[256,8192]{1,0:T(8,128)(2,1)} %x_hbm.1, bf16[8192,256]{1,0:T(8,128)(2,1)} %w_hbm.1, bf16[72,16,256]{2,1,0:T(8,128)(2,1)} %bitcast.11, bf16[256,1024]{1,0:T(8,128)(2,1)} %cot.1, s32[256]{0:T(256)} %tenant.1, ...), custom_call_target="tpu_custom_call" | custom-call | flops 8999999488 | bytes 30000000 | tf_op jit(solution)/shard_map/pallas_call | solution.py:470
  123.7 1.9 %copy.21 = bf16[256,1024]{1,0:T(8,128)(2,1)} copy(bf16[256,1024]{1,0:T(8,128)(2,1)} %get-tuple-element.13) | data formatting | bytes 1048576
  125.5 0.0 copy-start
  125.5 0.0 copy-start.1
  125.5 4.7 %copy.22 = bf16[256,8192]{1,0:T(8,128)(2,1)} copy(bf16[256,8192]{1,0:T(8,128)(2,1)} %get-tuple-element.14) | data formatting | bytes 8388608
  130.3 0.0 copy-done
  130.3 1.0 copy.23
  131.2 0.0 copy-done.1
  131.2 0.7 copy.24
  (1 shorter events, 0.0 us)
Async XLA Ops:
  125.5 4.7 %copy-start = (f32[256,1024]{1,0:T(8,128)S(1)}, f32[256,1024]{1,0:T(8,128)}, u32[]{:S(2)}) copy-start(f32[256,1024]{1,0:T(8,128)} %get-tuple-element.15) | copy-start | bytes 3145732
  125.5 5.7 %copy-start.1 = (f32[32,1024]{1,0:T(8,128)S(1)}, f32[32,1024]{1,0:T(8,128)}, u32[]{:S(2)}) copy-start(f32[32,1024]{1,0:T(8,128)} %get-tuple-element.16) | copy-start | bytes 393220

commit v2 on v1

v2 whole, which is shorter than its diff:
```python
import jax
import jax.numpy as jnp
from jax import lax
from jax.experimental import pallas as pl
from jax.experimental.pallas import tpu as pltpu
from jax.sharding import PartitionSpec as P

RANK = 16
BLOCK = 128
SCALE = 2.0
BF = jnp.bfloat16
F32 = jnp.float32
NT = (((1,), (1,)), ((), ()))
TN = (((0,), (0,)), ((), ()))


def mm(a, b, dims=(((1,), (0,)), ((), ()))):
    return lax.dot_general(a, b, dims, preferred_element_type=F32)


def iota(shape, dim):
    return lax.broadcasted_iota(jnp.int32, shape, dim)


def pick(cond):
    return jnp.where(cond, 1.0, 0.0).astype(BF)


def kernel(
    x_hbm,
    w_hbm,
    down,
    upmap,
    cot,
    tenant,
    fill,
    where,
    values,
    tgrad,
    gdown,
    gup,
    xv,
    wall,
    go,
    va,
    tga,
    tg_v,
    ab0,
    ab1,
    send_0,
    send_1,
    vb,
    send_b,
    at,
    recv_b,
    bt,
    gs,
    us,
    ur,
    te0,
    te1,
    lo,
    ri_s,
    rg_s,
    onehot,
    acc,
    cnt,
    loc,
    ab_sem,
    wy_sem,
    wx_sem,
    wc_sem,
    p0_sem,
    p1_sem,
    pb_sem,
    g0_sem,
    g1_sem,
    gu_sem,
    gy_sem,
):
    f = lax.axis_index("fsdp")
    t = lax.axis_index("tok")
    x = t // 8
    z = (t // 2) % 4
    c = t % 2

    def up(i, d):
        return lax.rem(i + d, 4)

    def dev_y(d):
        return (up(f, d), t)

    def dev_x(d):
        return (f, up(x, d) * 8 + z * 2 + c)

    def dev_z(d):
        return (f, x * 8 + up(z, d) * 2 + c)

    sibling = (f, x * 8 + z * 2 + (1 - c))

    def remote(src, dst, sem, i, dev):
        return pltpu.make_async_remote_copy(
            src_ref=src,
            dst_ref=dst,
            send_sem=sem.at[0, i],
            recv_sem=sem.at[1, i],
            device_id=dev,
            device_id_type=pl.DeviceIdType.MESH,
        )

    def my_cols(i, n):
        return pl.ds(pl.multiple_of(i * n, n), n)

    barrier = pltpu.get_barrier_semaphore()
    for d in (1, 3):
        pl.semaphore_signal(
            barrier, inc=1, device_id=dev_y(d), device_id_type=pl.DeviceIdType.MESH
        )

    def greet(d, carry):
        pl.semaphore_signal(
            barrier,
            inc=1,
            device_id=(f, lax.rem(t + d, 32)),
            device_id_type=pl.DeviceIdType.MESH,
        )
        return carry

    lax.fori_loop(1, 32, greet, 0)

    get_x = pltpu.make_async_copy(x_hbm, xv, loc.at[0])
    get_w = pltpu.make_async_copy(w_hbm, wall.at[f], loc.at[1])
    get_x.start()
    get_w.start()

    ab0[pl.ds(f * 80, 64)] = down[0:128, :].astype(F32).T.astype(BF).reshape(64, 16, 128)
    ab1[pl.ds(f * 64, 64)] = down[128:256, :].astype(F32).T.astype(BF).reshape(64, 16, 128)
    side = jnp.zeros((16, 16, 128), F32)
    for g in range(4):
        place = pick(iota((32, 128), 1) == iota((32, 128), 0) + 32 * g)
        moved = mm(upmap[...], place, TN).reshape(16, 64, 128)
        side = side + moved[:, g * 16 : (g + 1) * 16, :]
    ab0[pl.ds(f * 80 + 64, 16)] = side.astype(BF)

    pl.semaphore_wait(barrier, 33)

    pending = []

    def ring_y(part_of, sem, n0):
        first = {}
        last = []

        def start():
            for i, (d, s) in enumerate(((1, 0), (3, 1), (1, 1), (3, 0))):
                cp = remote(part_of(f, s), part_of(f, s), sem, n0 + i, dev_y(d))
                cp.start()
                first[d, s] = cp
                pending.append(cp)

        def forward():
            for i, (d, s) in enumerate(((1, 0), (3, 1))):
                first[d, s].wait_recv()
                src = up(f, 4 - d)
                cp = remote(
                    part_of(src, s), part_of(src, s), sem, n0 + 4 + i, dev_y(d)
                )
                cp.start()
                last.append(cp)
                pending.append(cp)

        def near():
            first[1, 1].wait_recv()
            first[3, 0].wait_recv()

        def far():
            for cp in last:
                cp.wait_recv()

        return start, forward, near, far

    p_start, p_forward, p_near, p_far = ring_y(
        lambda i, s: ab0.at[pl.ds(i * 80 + s * 40, 40)], ab_sem, 0
    )
    q_start, q_forward, q_near, q_far = ring_y(
        lambda i, s: ab1.at[pl.ds(i * 64 + s * 32, 32)], ab_sem, 6
    )
    p_start()

    b0 = (f * 32 + t) * 2

    def used_rows():
        rows = iota((256, 1), 0)
        return rows < jnp.where(rows < BLOCK, fill[b0], fill[b0 + 1] + BLOCK)

    used = used_rows()
    for j in range(4):
        go[j] = jnp.where(used, cot[:, j * 256 : (j + 1) * 256].astype(F32), 0.0).astype(BF)
    va[...] = jnp.zeros_like(va)
    get_x.wait()
    get_w.wait()

    def own_step(k, carry):
        cols = my_cols(k, 256)
        wk = wall[f, cols, :]
        va[f] += mm(xv[:, cols], wk)
        tga[:, cols] = mm(go[f], wk, NT)
        return carry

    p_forward()
    q_start()
    lax.fori_loop(0, 12, own_step, 0)
    p_near()
    p_far()

    lane32 = iota((16, 128), 1) >> 5

    def pick_0(b, carry):
        dst = my_cols(b, 16)
        send_0[dst, :] = ab0[where[0, f * 64 + b]]
        v = ab0[where[1, f * 64 + b]]
        vb[dst, :] = jnp.where(lane32 == where[2, f * 64 + b], v.astype(F32), 0.0).astype(BF)
        return carry

    def pick_1(b, carry):
        send_1[my_cols(b, 16), :] = ab1[where[3, f * 64 + b]]
        return carry

    el = iota((128, 128), 0)
    ej = iota((128, 128), 1)

    def swap_0(d):
        to = lax.rem(t + d, 32)
        return (
            remote(send_0.at[my_cols(to, 32), :], at.at[:, my_cols(t * 2, 128)], p0_sem, d, (f, to)),
            remote(send_b.at[my_cols(to, 32), :], recv_b.at[t], pb_sem, d, (f, to)),
        )

    def swap_1(d):
        to = lax.rem(t + d, 32)
        return (
            remote(
                send_1.at[my_cols(to, 32), :], at.at[:, my_cols(t * 2 + 1, 128)], p1_sem, d, (f, to)
            ),
        )

    def over_tok(copies, act):
        def step(d, carry):
            for cp in copies(d):
                if act == "start":
                    cp.start()
                elif act == "recv":
                    cp.wait_recv()
                else:
                    cp.wait_send()
            return carry

        lax.fori_loop(1, 32, step, 0)

    lax.fori_loop(0, 64, pick_0, 0)
    spread = pick(((el & 31) == (ej & 31)) & ((ej >> 5) == (t & 3)))
    send_b[...] = mm(vb[...], spread).astype(BF)
    over_tok(swap_0, "start")
    q_forward()

    base = (x * 1024 + c * 512, 4096 + z * 1024 + c * 512)

    def wslice(fi, row0):
        return wall.at[fi, pl.ds(pl.multiple_of(row0, 256), 256), :]

    wy = {}
    n_y = 0
    for h in range(2):
        for d, s in ((1, 0), (3, 1), (1, 1), (3, 0)):
            r0 = base[h] + s * 256
            cp = remote(
                w_hbm.at[pl.ds(pl.multiple_of(r0, 256), 256), :],
                wslice(f, r0),
                wy_sem,
                n_y,
                dev_y(d),
            )
            cp.start()
            wy[h, d, s] = cp
            pending.append(cp)
            n_y += 1

    at[:, my_cols(t * 2, 128)] = send_0[my_cols(t, 32), :]
    recv_b[t] = send_b[my_cols(t, 32), :]
    q_near()
    q_far()
    lax.fori_loop(0, 64, pick_1, 0)
    over_tok(swap_1, "start")
    at[:, my_cols(t * 2 + 1, 128)] = send_1[my_cols(t, 32), :]

    lax.fori_loop(12, 32, own_step, 0)

    wx = {}
    counters = {"x": 0, "c": 0}
    wc = {}
    foreign = (up(f, 3), up(f, 1), up(f, 2))

    def to_sibling(fi, r0, key):
        cp = remote(wslice(fi, r0), wslice(fi, r0), wc_sem, counters["c"], sibling)
        counters["c"] += 1
        cp.start()
        wc[key] = cp
        pending.append(cp)

    def to_plane(fi, r0, d, key, h):
        cp = remote(
            wslice(fi, r0), wslice(fi, r0), wx_sem, counters["x"], (dev_x if h == 0 else dev_z)(d)
        )
        counters["x"] += 1
        cp.start()
        wx[key] = cp
        pending.append(cp)

    fw = {}

    def w_near(h):
        nonlocal n_y
        for d, s in ((1, 0), (3, 1)):
            wy[h, d, s].wait_recv()
            src = up(f, 4 - d)
            r0 = base[h] + s * 256
            cp = remote(wslice(src, r0), wslice(src, r0), wy_sem, n_y, dev_y(d))
            n_y += 1
            cp.start()
            fw[h, s] = cp
            pending.append(cp)
        for d, s in ((1, 0), (3, 1), (1, 1), (3, 0)):
            if (d, s) in ((1, 1), (3, 0)):
                wy[h, d, s].wait_recv()
            fi = 0 if d == 1 else 1
            r0 = base[h] + s * 256
            for dd in (1, 3) if s == 0 else (3, 1):
                to_plane(foreign[fi], r0, dd, (h, dd, fi, s), h)
            to_sibling(foreign[fi], r0, (h, 0, fi, s))

    def w_far(h):
        for s in range(2):
            fw[h, s].wait_recv()
            r0 = base[h] + s * 256
            for dd in (1, 3) if s == 0 else (3, 1):
                to_plane(foreign[2], r0, dd, (h, dd, 2, s), h)
            to_sibling(foreign[2], r0, (h, 0, 2, s))

    def here(h, d):
        if h == 0:
            return up(x, d) * 1024 + c * 512
        return 4096 + up(z, d) * 1024 + c * 512

    def w_along(h, fi):
        for d, s in ((1, 0), (3, 1)):
            wx[h, d, fi, s].wait_recv()
            r0 = here(h, 4 - d) + s * 256
            to_plane(foreign[fi], r0, d, (h, 2, fi, s), h)
            to_sibling(foreign[fi], r0, (h, d, fi, s))
        for d, s in ((1, 1), (3, 0)):
            wx[h, d, fi, s].wait_recv()
            r0 = here(h, 4 - d) + s * 256
            to_sibling(foreign[fi], r0, (h, d, fi, s))

    w_near(0)

    tlane = (iota((1, 1024), 1) >> 4) + f * 64

    def count_step(b, total):
        return total + jnp.where(tlane == tenant[b], fill[b].astype(F32), 0.0)

    cnt[...] = lax.fori_loop(0, 256, count_step, jnp.zeros((1, 1024), F32))

    over_tok(swap_0, "recv")
    for q in range(8):
        total = recv_b[4 * q]
        for i in range(1, 4):
            total = total + recv_b[4 * q + i]
        bt[:, q * 128 : (q + 1) * 128] = total
    diagonal = (iota((256, 32), 0) >> 7) == (iota((256, 32), 1) >> 4)
    rank_grad = jnp.zeros((256, 32), F32)
    for j in range(4):
        rank_grad = rank_grad + mm(go[j], bt[:, j * 256 : (j + 1) * 256], NT)
    rg_s[...] = jnp.where(diagonal, SCALE * rank_grad, 0.0).astype(BF)

    def terms_step(k, carry):
        cols = my_cols(k, 1024)
        gs[:, cols] = mm(rg_s[...], xv[:, cols], TN).astype(BF)
        return carry

    lax.fori_loop(0, 8, terms_step, 0)

    def back_0(d):
        to = lax.rem(t + d, 32)
        return (
            remote(gs.at[:, my_cols(to * 2, 128)], te0.at[f, my_cols(t, 32), :], g0_sem, d, (f, to)),
        )

    def back_1(d):
        to = lax.rem(t + d, 32)
        return (
            remote(
                gs.at[:, my_cols(to * 2 + 1, 128)], te1.at[f, my_cols(t, 32), :], g1_sem, d, (f, to)
            ),
            remote(us.at[:, my_cols(to // 4, 128)], ur.at[my_cols(t, 32), :], gu_sem, d, (f, to)),
        )

    over_tok(back_0, "start")
    te0[f, my_cols(t, 32), :] = gs[:, my_cols(t * 2, 128)]

    over_tok(swap_1, "recv")

    def rank_step(k, total):
        cols = my_cols(k, 1024)
        return total + mm(xv[:, cols], at[:, cols], NT)

    rank_in = lax.fori_loop(0, 8, rank_step, jnp.zeros((256, 32), F32))
    ri_s[...] = jnp.where(diagonal, rank_in, 0.0).astype(BF)
    for j in range(4):
        us[:, j * 256 : (j + 1) * 256] = (SCALE * mm(ri_s[...], go[j], TN)).astype(BF)
    over_tok(back_1, "start")
    te1[f, my_cols(t, 32), :] = gs[:, my_cols(t * 2 + 1, 128)]
    ur[my_cols(t, 32), :] = us[:, my_cols(t // 4, 128)]

    w_near(1)
    w_far(0)

    u_start, u_forward, u_near, u_far = ring_y(
        lambda i, s: te0.at[i, pl.ds(s * 512, 512)], gy_sem, 0
    )
    v_start, v_forward, v_near, v_far = ring_y(
        lambda i, s: te1.at[i, pl.ds(s * 640, 640)], gy_sem, 6
    )
    over_tok(back_0, "recv")
    u_start()

    w_far(1)
    for h in range(2):
        w_along(h, 0)

    over_tok(back_1, "recv")
    packed = jnp.zeros((256, 128), F32)
    for q in range(4):
        e = pick(((el >> 5) == (t & 3)) & ((ej >> 5) == q) & ((el & 31) == (ej & 31)))
        packed = packed + mm(ur[q * 256 : (q + 1) * 256, :], e)
    te1[f, 1024:1280, :] = packed.astype(BF)
    u_forward()
    v_start()

    for h in range(2):
        w_along(h, 1)

    for j in range(4):
        lo[:, j * 256 : (j + 1) * 256] = (
            SCALE * mm(ri_s[...], bt[:, j * 256 : (j + 1) * 256])
        ).astype(BF)

    def tile(row0):
        cols = pl.ds(pl.multiple_of(row0, 256), 256)
        xk = xv[:, cols]
        total = tga[:, cols] + mm(rg_s[...], at[:, cols])
        for fi in foreign:
            wk = wall[fi, cols, :]
            va[fi] += mm(xk, wk)
            total = total + mm(go[fi], wk, NT)
        tg_v[:, cols] = total.astype(BF)
        pltpu.make_async_copy(tg_v.at[:, cols], tgrad.at[:, cols], loc.at[2]).start()

    def tiles(d):
        def step(i, carry):
            h = i // 4
            pos = jnp.where(h == 0, lax.rem(x + d, 4), lax.rem(z + d, 4))
            tile(h * 4096 + pos * 1024 + (i % 4) * 256)
            return carry

        lax.fori_loop(0, 8, step, 0)

    def await_sibling(d):
        for h in range(2):
            for fi in range(3):
                for s in range(2):
                    wc[h, d, fi, s].wait_recv()

    await_sibling(0)
    tiles(0)
    u_near()
    v_forward()
    for h in range(2):
        w_along(h, 2)

    shift = iota((16, 1024), 1) - iota((16, 1024), 0) + f * 1024
    acc[...] = jnp.zeros_like(acc)

    def reduce_group(fi):
        def step(q, carry):
            for i in range(8):
                key = tenant[fi * 64 + q * 8 + i] * 16
                onehot[i * 16 : (i + 1) * 16, :] = pick(shift == key)
            unpack = pick((el == (q // 2) * 32 + ej) & (ej < 32))
            u = mm(te1[fi, my_cols(8 + q % 2, 128), :], unpack).astype(BF)
            lhs = jnp.concatenate(
                [te0[fi, my_cols(q, 128), :], te1[fi, my_cols(q, 128), :], u], axis=1
            )
            acc[...] += mm(lhs, onehot[...], TN)
            return carry

        lax.fori_loop(0, 8, step, 0)

    reduce_group(f)
    await_sibling(1)
    tiles(3)
    await_sibling(3)
    tiles(1)
    for fi in range(3):
        for h in range(2):
            for s in range(2):
                wx[h, 2, fi, s].wait_recv()
                to_sibling(foreign[fi], here(h, 2) + s * 256, (h, 2, fi, s))
    v_near()
    reduce_group(foreign[0])
    reduce_group(foreign[1])
    await_sibling(2)
    tiles(2)
    used = used_rows()
    for j in range(4):
        cols = slice(j * 256, (j + 1) * 256)
        values[:, cols] = jnp.where(used, va[j] + lo[:, cols].astype(F32), 0.0).astype(BF)
    u_far()
    v_far()
    reduce_group(foreign[2])
    denom = jnp.maximum(cnt[...], 1.0)
    gdown[...] = acc[0:256, :] / denom
    gup[...] = acc[256:288, :] / denom

    pltpu.make_async_copy(tg_v, tgrad, loc.at[2]).wait()
    for copies in (swap_0, swap_1, back_0, back_1):
        over_tok(copies, "sent")
    for cp in pending:
        cp.wait_send()


def hand_on(v_in, t_in, d_in, u_in, v_out, t_out, d_out, u_out, sem):
    copies = [(v_in, v_out), (d_in, d_out), (u_in, u_out)]
    for i in range(8):
        rows = pl.ds(i * 32, 32)
        copies.append((t_in.at[rows, :], t_out.at[rows, :]))
    copies = [
        pltpu.make_async_copy(a, b, sem.at[i]) for i, (a, b) in enumerate(copies)
    ]
    for cp in copies:
        cp.start()
    for cp in copies:
        cp.wait()


def local(tokens, weight, down, up, cotangent, tenant, fill):
    owner, slot = tenant // 64, tenant % 64
    where = jnp.stack(
        [owner * 80 + slot, owner * 80 + 64 + slot // 4, slot % 4, owner * 64 + slot]
    )
    any_ = pl.BlockSpec(memory_space=pl.ANY)
    vmem = pl.BlockSpec(memory_space=pltpu.VMEM)
    smem = pl.BlockSpec(memory_space=pltpu.SMEM)
    dma = pltpu.SemaphoreType.DMA
    V = pltpu.VMEM
    out_shape = (
        jax.ShapeDtypeStruct((256, 1024), BF),
        jax.ShapeDtypeStruct((256, 8192), BF),
        jax.ShapeDtypeStruct((256, 1024), F32),
        jax.ShapeDtypeStruct((32, 1024), F32),
    )
    outs = pl.pallas_call(
        kernel,
        out_shape=out_shape,
        in_specs=[any_, any_, vmem, vmem, vmem, smem, smem, smem],
        out_specs=(vmem, any_, vmem, vmem),
        scratch_shapes=[
            V((256, 8192), BF),
            V((4, 8192, 256), BF),
            V((4, 256, 256), BF),
            V((4, 256, 256), F32),
            V((256, 8192), F32),
            V((256, 8192), BF),
            V((320, 16, 128), BF),
            V((256, 16, 128), BF),
            V((1024, 128), BF),
            V((1024, 128), BF),
            V((1024, 128), BF),
            V((1024, 128), BF),
            V((32, 8192), BF),
            V((32, 32, 128), BF),
            V((32, 1024), BF),
            V((32, 8192), BF),
            V((32, 1024), BF),
            V((1024, 128), BF),
            V((4, 1024, 128), BF),
            V((4, 1280, 128), BF),
            V((256, 1024), BF),
            V((256, 32), BF),
            V((256, 32), BF),
            V((128, 1024), BF),
            V((384, 1024), F32),
            V((1, 1024), F32),
            dma((3,)),
            dma((2, 12)),
            dma((2, 12)),
            dma((2, 36)),
            dma((2, 48)),
            dma((2, 32)),
            dma((2, 32)),
            dma((2, 32)),
            dma((2, 32)),
            dma((2, 32)),
            dma((2, 32)),
            dma((2, 12)),
        ],
        compiler_params=pltpu.CompilerParams(
            has_side_effects=True, collective_id=1, vmem_limit_bytes=60 * 1024 * 1024
        ),
        cost_estimate=pl.CostEstimate(
            flops=9_000_000_000, bytes_accessed=30_000_000, transcendentals=0
        ),
    )(tokens, weight, down, up, cotangent, tenant, fill, where)
    return pl.pallas_call(
        hand_on,
        out_shape=out_shape,
        in_specs=[any_] * 4,
        out_specs=(any_,) * 4,
        scratch_shapes=[dma((11,))],
    )(*outs)


def solution(mesh):
    placed = (
        P(("fsdp", "tok"), None),
        P(None, "fsdp"),
        P("tok", "fsdp"),
        P("tok", "fsdp"),
        P(("fsdp", "tok"), None),
        P(),
        P(),
    )
    return jax.shard_map(
        local,
        mesh=mesh,
        in_specs=placed,
        out_specs=(
            P(("fsdp", "tok"), None),
            P(("fsdp", "tok"), None),
            P("tok", "fsdp"),
            P("tok", "fsdp"),
        ),
        check_vma=False,
    )
```

time: 132 us -> 289 us (2.19)
  Pallas kernels: 118 us -> 286 us
  local copies, waits for them, and re-layouts: 10.7 us -> 0 us
    pallas_call x1 -> x2, Pallas kernels: 118 us -> 286 us  [the longest x1 180 us: local(): pl.pallas_call(hand_on, out_shape=out_shape, in_specs=[any_] * 4, out_spe...]
    unnamed x9 -> x0, local copies, waits for them, and re-layouts: 9.24 us -> none
where the time goes in v2:
time: 289 us; the launch traced here: 288 us
  Pallas kernels  286 us (99%)
    pallas_call x1, Pallas kernels, local(): pl.pallas_call(hand_on, out_shape=out_shape, in_specs=[any_] * 4, out_spe...  180 us
    pallas_call x1, Pallas kernels, local(): pl.pallas_call(kernel, out_shape=out_shape, in_specs=[any_, any_, vmem, v...  106 us

profile of v2, /device:TPU:1, one launch (start us, length us, event | category | flops | bytes accessed | tf_op | source)
XLA Modules:
  0.0 288.3 jit_solution(12882404532399656550)
XLA Ops:
  0.6 0.7 multiply_add_fusion.1
  1.3 0.6 pad_add_fusion.where
  1.9 106.5 %shard_map.102 = (bf16[256,1024]{1,0:T(8,128)(2,1)}, bf16[256,8192]{1,0:T(8,128)(2,1)}, f32[256,1024]{1,0:T(8,128)}, f32[32,1024]{1,0:T(8,128)}) custom-call(bf16[256,8192]{1,0:T(8,128)(2,1)} %x_hbm.1, bf16[8192,256]{1,0:T(8,128)(2,1)} %w_hbm.1, bf16[256,1024]{1,0:T(8,128)(2,1)} %down.1, bf16[32,1024]{1,0:T(8,128)(2,1)} %upmap.1, bf16[256,1024]{1,0:T(8,128)(2,1)} %cot.1, ...), custom_call_target="tpu_custom_call" | custom-call | flops 8999999488 | bytes 30000000 | tf_op jit(solution)/shard_map/pallas_call | solution.py:571
  108.4 179.9 %shard_map.103 = (bf16[256,1024]{1,0:T(8,128)(2,1)}, bf16[256,8192]{1,0:T(8,128)(2,1)}, f32[256,1024]{1,0:T(8,128)}, f32[32,1024]{1,0:T(8,128)}) custom-call(bf16[256,1024]{1,0:T(8,128)(2,1)} %get-tuple-element.8.v_in, bf16[256,8192]{1,0:T(8,128)(2,1)} %get-tuple-element.9.t_in, f32[256,1024]{1,0:T(8,128)} %get-tuple-element.10.d_in, ...), custom_call_target="tpu_custom_call" | custom-call | tf_op jit(solution)/shard_map/pallas_call | solution.py:623
  (1 shorter events, 0.0 us)

commit v3 on v2

v3 whole, which is shorter than its diff:
```python
import jax
import jax.numpy as jnp
from jax import lax
from jax.experimental import pallas as pl
from jax.experimental.pallas import tpu as pltpu
from jax.sharding import PartitionSpec as P

RANK = 16
BLOCK = 128
SCALE = 2.0
BF = jnp.bfloat16
F32 = jnp.float32
NT = (((1,), (1,)), ((), ()))
TN = (((0,), (0,)), ((), ()))


def mm(a, b, dims=(((1,), (0,)), ((), ()))):
    return lax.dot_general(a, b, dims, preferred_element_type=F32)


def iota(shape, dim):
    return lax.broadcasted_iota(jnp.int32, shape, dim)


def pick(cond):
    return jnp.where(cond, 1.0, 0.0).astype(BF)


def kernel(
    x_hbm,
    w_hbm,
    down,
    upmap,
    cot,
    tenant,
    fill,
    where,
    values,
    tgrad,
    te_out,
    tu_out,
    xv,
    wall,
    go,
    va,
    tga,
    tg_v,
    ab_a,
    ab_b,
    send_a,
    vb,
    send_b,
    at,
    recv_b,
    bt,
    gs,
    us,
    ur,
    te,
    tu,
    lo,
    ri_s,
    rg_s,
    loc,
    y_sem,
    wy_sem,
    wl_sem,
    wx_sem,
    wc_sem,
    pa_sem,
    pb_sem,
    gt_sem,
    gu_sem,
):
    f = lax.axis_index("fsdp")
    t = lax.axis_index("tok")
    x = t // 8
    z = (t // 2) % 4
    c = t % 2

    def up(i, d):
        return lax.rem(i + d, 4)

    def dev_y(d):
        return (up(f, d), t)

    def dev_x(d):
        return (f, up(x, d) * 8 + z * 2 + c)

    def dev_z(d):
        return (f, x * 8 + up(z, d) * 2 + c)

    sibling = (f, x * 8 + z * 2 + (1 - c))

    def remote(src, dst, sem, i, dev):
        return pltpu.make_async_remote_copy(
            src_ref=src,
            dst_ref=dst,
            send_sem=sem.at[0, i],
            recv_sem=sem.at[1, i],
            device_id=dev,
            device_id_type=pl.DeviceIdType.MESH,
        )

    def my_cols(i, n):
        return pl.ds(pl.multiple_of(i * n, n), n)

    barrier = pltpu.get_barrier_semaphore()
    for d in (1, 3):
        pl.semaphore_signal(
            barrier, inc=1, device_id=dev_y(d), device_id_type=pl.DeviceIdType.MESH
        )

    def greet(d, carry):
        pl.semaphore_signal(
            barrier,
            inc=1,
            device_id=(f, lax.rem(t + d, 32)),
            device_id_type=pl.DeviceIdType.MESH,
        )
        return carry

    lax.fori_loop(1, 32, greet, 0)

    get_x = pltpu.make_async_copy(x_hbm, xv, loc.at[0])
    get_w = pltpu.make_async_copy(w_hbm, wall.at[f], loc.at[1])
    get_x.start()
    get_w.start()

    side = jnp.zeros((16, 16, 128), F32)
    for g in range(4):
        place = pick(iota((32, 128), 1) == iota((32, 128), 0) + 32 * g)
        moved = mm(upmap[...], place, TN).reshape(16, 64, 128)
        side = side + moved[:, g * 16 : (g + 1) * 16, :]
    ab_b[pl.ds(f * 16, 16)] = side.astype(BF)
    ab_a[pl.ds(f * 64, 64)] = down[...].astype(F32).T.astype(BF).reshape(64, 16, 256)

    pl.semaphore_wait(barrier, 33)

    pending = []

    def ring_y(part_of, sem, n0):
        first = {}
        last = []

        def start():
            for i, (d, s) in enumerate(((1, 0), (3, 1), (1, 1), (3, 0))):
                cp = remote(part_of(f, s), part_of(f, s), sem, n0 + i, dev_y(d))
                cp.start()
                first[d, s] = cp
                pending.append(cp)

        def forward():
            for i, (d, s) in enumerate(((1, 0), (3, 1))):
                first[d, s].wait_recv()
                src = up(f, 4 - d)
                cp = remote(
                    part_of(src, s), part_of(src, s), sem, n0 + 4 + i, dev_y(d)
                )
                cp.start()
                last.append(cp)
                pending.append(cp)

        def near():
            first[1, 1].wait_recv()
            first[3, 0].wait_recv()

        def far():
            for cp in last:
                cp.wait_recv()

        return start, forward, near, far

    b_start, b_forward, b_near, b_far = ring_y(
        lambda i, s: ab_b.at[pl.ds(i * 16 + s * 8, 8)], y_sem, 0
    )
    a_start, a_forward, a_near, a_far = ring_y(
        lambda i, s: ab_a.at[pl.ds(i * 64 + s * 32, 32)], y_sem, 6
    )
    t_start, t_forward, t_near, t_far = ring_y(
        lambda i, s: te.at[i, pl.ds(s * 512, 512)], y_sem, 12
    )
    u_start, u_forward, u_near, u_far = ring_y(
        lambda i, s: tu.at[i, pl.ds(s * 128, 128)], y_sem, 18
    )
    b_start()

    base = (x * 1024 + c * 512, 4096 + z * 1024 + c * 512)
    pos1 = (z, x)
    dev1 = (dev_z, dev_x)
    dev2 = (dev_x, dev_z)

    def wslice(fi, row0, n):
        return wall.at[fi, pl.ds(pl.multiple_of(row0, 64), n), :]

    def sub_at(h, d):
        return base[h] + up(pos1[h], d) * 128

    wy = {}
    n_y = 0
    for h in range(2):
        for d, s in ((1, 0), (3, 1), (1, 1), (3, 0)):
            r0 = sub_at(h, 0) + s * 64
            cp = remote(
                w_hbm.at[pl.ds(pl.multiple_of(r0, 64), 64), :],
                wslice(f, r0, 64),
                wy_sem,
                n_y,
                dev_y(d),
            )
            cp.start()
            wy[h, d, s] = cp
            pending.append(cp)
            n_y += 1
    a_start()

    b0 = (f * 32 + t) * 2

    def used_rows():
        rows = iota((256, 1), 0)
        return rows < jnp.where(rows < BLOCK, fill[b0], fill[b0 + 1] + BLOCK)

    used = used_rows()
    for j in range(4):
        go[j] = jnp.where(used, cot[:, j * 256 : (j + 1) * 256].astype(F32), 0.0).astype(BF)

    b_forward()
    va[...] = jnp.zeros_like(va)
    b_near()

    wl = {}
    wx = {}
    wc = {}
    fw = {}
    counters = {"l": 0, "x": 0, "c": 0}
    foreign = (up(f, 3), up(f, 1), up(f, 2))

    def same_place(fi, r0, n, sem, kind, dev):
        cp = remote(wslice(fi, r0, n), wslice(fi, r0, n), sem, counters[kind], dev)
        counters[kind] += 1
        cp.start()
        pending.append(cp)
        return cp

    def to_sibling(fi, r0, key):
        wc[key] = same_place(fi, r0, 256, wc_sem, "c", sibling)

    def w_near(h):
        nonlocal n_y
        for d, s in ((1, 0), (3, 1)):
            wy[h, d, s].wait_recv()
            src = up(f, 4 - d)
            r0 = sub_at(h, 0) + s * 64
            cp = remote(wslice(src, r0, 64), wslice(src, r0, 64), wy_sem, n_y, dev_y(d))
            n_y += 1
            cp.start()
            fw[h, s] = cp
            pending.append(cp)
        for d, s in ((1, 1), (3, 0)):
            wy[h, d, s].wait_recv()
        for fi in range(2):
            for dd in (1, 3):
                wl[h, dd, fi] = same_place(
                    foreign[fi], sub_at(h, 0), 128, wl_sem, "l", dev1[h](dd)
                )

    def w_far(h):
        for s in range(2):
            fw[h, s].wait_recv()
        for dd in (1, 3):
            wl[h, dd, 2] = same_place(
                foreign[2], sub_at(h, 0), 128, wl_sem, "l", dev1[h](dd)
            )

    def w_line(h, fi):
        for d, s in ((1, 0), (3, 1)):
            wl[h, d, fi].wait_recv()
            wl[h, 2, fi, s] = same_place(
                foreign[fi], sub_at(h, 4 - d) + s * 64, 64, wl_sem, "l", dev1[h](d)
            )

    def to_plane(fi, r0, d, key, h):
        wx[key] = same_place(fi, r0, 256, wx_sem, "x", dev2[h](d))

    def w_plane(h, fi):
        for s in range(2):
            wl[h, 2, fi, s].wait_recv()
        for s in range(2):
            r0 = base[h] + s * 256
            for dd in (1, 3) if s == 0 else (3, 1):
                to_plane(foreign[fi], r0, dd, (h, dd, fi, s), h)
        for s in range(2):
            to_sibling(foreign[fi], base[h] + s * 256, (h, 0, fi, s))

    def here(h, d):
        if h == 0:
            return up(x, d) * 1024 + c * 512
        return 4096 + up(z, d) * 1024 + c * 512

    def w_along(h, fi):
        for d, s in ((1, 0), (3, 1)):
            wx[h, d, fi, s].wait_recv()
            r0 = here(h, 4 - d) + s * 256
            to_plane(foreign[fi], r0, d, (h, 2, fi, s), h)
            to_sibling(foreign[fi], r0, (h, d, fi, s))
        for d, s in ((1, 1), (3, 0)):
            wx[h, d, fi, s].wait_recv()
            r0 = here(h, 4 - d) + s * 256
            to_sibling(foreign[fi], r0, (h, d, fi, s))

    b_far()

    lane32 = iota((16, 128), 1) >> 5
    el = iota((128, 128), 0)
    ej = iota((128, 128), 1)

    def pick_b(b, carry):
        v = ab_b[where[0, f * 64 + b]]
        vb[my_cols(b, 16), :] = jnp.where(
            lane32 == where[1, f * 64 + b], v.astype(F32), 0.0
        ).astype(BF)
        return carry

    def pick_a(b, carry):
        send_a[my_cols(b, 16), :] = ab_a[tenant[f * 64 + b]]
        return carry

    def swap_a(d):
        to = lax.rem(t + d, 32)
        return remote(
            send_a.at[my_cols(to, 32), :], at.at[:, my_cols(t, 256)], pa_sem, d, (f, to)
        )

    def swap_b(d):
        to = lax.rem(t + d, 32)
        return remote(send_b.at[my_cols(to, 32), :], recv_b.at[t], pb_sem, d, (f, to))

    def back_t(d):
        to = lax.rem(t + d, 32)
        return remote(
            gs.at[:, my_cols(to, 256)], te.at[f, my_cols(t, 32), :], gt_sem, d, (f, to)
        )

    def back_u(d):
        to = lax.rem(t + d, 32)
        return remote(
            us.at[:, my_cols(to // 4, 128)], ur.at[my_cols(t, 32), :], gu_sem, d, (f, to)
        )

    def over_tok(copy, act):
        def step(d, carry):
            cp = copy(d)
            if act == "start":
                cp.start()
            elif act == "recv":
                cp.wait_recv()
            else:
                cp.wait_send()
            return carry

        lax.fori_loop(1, 32, step, 0)

    lax.fori_loop(0, 64, pick_b, 0)
    spread = pick(((el & 31) == (ej & 31)) & ((ej >> 5) == (t & 3)))
    send_b[...] = mm(vb[...], spread).astype(BF)
    over_tok(swap_b, "start")
    recv_b[t] = send_b[my_cols(t, 32), :]

    get_x.wait()
    w_near(0)
    w_near(1)

    over_tok(swap_b, "recv")
    for q in range(8):
        total = recv_b[4 * q]
        for i in range(1, 4):
            total = total + recv_b[4 * q + i]
        bt[:, q * 128 : (q + 1) * 128] = total
    diagonal = (iota((256, 32), 0) >> 7) == (iota((256, 32), 1) >> 4)
    rank_grad = jnp.zeros((256, 32), F32)
    for j in range(4):
        rank_grad = rank_grad + mm(go[j], bt[:, j * 256 : (j + 1) * 256], NT)
    rg_s[...] = jnp.where(diagonal, SCALE * rank_grad, 0.0).astype(BF)

    def terms_step(k, carry):
        cols = my_cols(k, 1024)
        gs[:, cols] = mm(rg_s[...], xv[:, cols], TN).astype(BF)
        return carry

    lax.fori_loop(0, 8, terms_step, 0)
    over_tok(back_t, "start")
    te[f, my_cols(t, 32), :] = gs[:, my_cols(t, 256)]

    w_far(0)
    w_far(1)
    for h in range(2):
        w_line(h, 0)
        w_line(h, 1)
    a_forward()
    get_w.wait()

    def own_step(k, carry):
        cols = my_cols(k, 256)
        wk = wall[f, cols, :]
        va[f] += mm(xv[:, cols], wk)
        tga[:, cols] = mm(go[f], wk, NT)
        return carry

    lax.fori_loop(0, 8, own_step, 0)
    for h in range(2):
        w_line(h, 2)
    for fi in range(2):
        for h in range(2):
            w_plane(h, fi)
    over_tok(back_t, "recv")
    t_start()
    put_own = pltpu.make_async_copy(te.at[f], te_out.at[f], loc.at[3])
    put_own.start()
    for h in range(2):
        w_plane(h, 2)
    a_near()
    a_far()
    lax.fori_loop(0, 64, pick_a, 0)
    over_tok(swap_a, "start")
    at[:, my_cols(t, 256)] = send_a[my_cols(t, 32), :]
    for h in range(2):
        w_along(h, 0)
    lax.fori_loop(8, 32, own_step, 0)
    t_forward()

    over_tok(swap_a, "recv")

    def rank_step(k, total):
        cols = my_cols(k, 1024)
        return total + mm(xv[:, cols], at[:, cols], NT)

    rank_in = lax.fori_loop(0, 8, rank_step, jnp.zeros((256, 32), F32))
    ri_s[...] = jnp.where(diagonal, rank_in, 0.0).astype(BF)
    for j in range(4):
        us[:, j * 256 : (j + 1) * 256] = (SCALE * mm(ri_s[...], go[j], TN)).astype(BF)
    over_tok(back_u, "start")
    ur[my_cols(t, 32), :] = us[:, my_cols(t // 4, 128)]

    for h in range(2):
        w_along(h, 1)
    for j in range(4):
        lo[:, j * 256 : (j + 1) * 256] = (
            SCALE * mm(ri_s[...], bt[:, j * 256 : (j + 1) * 256])
        ).astype(BF)

    over_tok(back_u, "recv")
    packed = jnp.zeros((256, 128), F32)
    for q in range(4):
        e = pick(((el >> 5) == (t & 3)) & ((ej >> 5) == q) & ((el & 31) == (ej & 31)))
        packed = packed + mm(ur[q * 256 : (q + 1) * 256, :], e)
    tu[f] = packed.astype(BF)
    u_start()

    def tile(row0):
        cols = pl.ds(pl.multiple_of(row0, 256), 256)
        xk = xv[:, cols]
        total = tga[:, cols] + mm(rg_s[...], at[:, cols])
        for fi in foreign:
            wk = wall[fi, cols, :]
            va[fi] += mm(xk, wk)
            total = total + mm(go[fi], wk, NT)
        tg_v[:, cols] = total.astype(BF)
        pltpu.make_async_copy(tg_v.at[:, cols], tgrad.at[:, cols], loc.at[2]).start()

    def tiles(d):
        def step(i, carry):
            h = i // 4
            pos = jnp.where(h == 0, lax.rem(x + d, 4), lax.rem(z + d, 4))
            tile(h * 4096 + pos * 1024 + (i % 4) * 256)
            return carry

        lax.fori_loop(0, 8, step, 0)

    def await_sibling(d):
        for h in range(2):
            for fi in range(3):
                for s in range(2):
                    wc[h, d, fi, s].wait_recv()

    for h in range(2):
        w_along(h, 2)
    await_sibling(0)
    tiles(0)
    u_forward()
    for fi in range(3):
        for h in range(2):
            for s in range(2):
                wx[h, 2, fi, s].wait_recv()
                to_sibling(foreign[fi], here(h, 2) + s * 256, (h, 2, fi, s))
    await_sibling(1)
    tiles(3)
    await_sibling(3)
    tiles(1)
    await_sibling(2)
    tiles(2)
    used = used_rows()
    for j in range(4):
        cols = slice(j * 256, (j + 1) * 256)
        values[:, cols] = jnp.where(used, va[j] + lo[:, cols].astype(F32), 0.0).astype(BF)
    t_near()
    t_far()
    puts = [put_own]
    for i, fi in enumerate(foreign):
        puts.append(pltpu.make_async_copy(te.at[fi], te_out.at[fi], loc.at[4 + i]))
        puts[-1].start()
    u_near()
    u_far()
    puts.append(pltpu.make_async_copy(tu, tu_out, loc.at[7]))
    puts[-1].start()

    pltpu.make_async_copy(tg_v, tgrad, loc.at[2]).wait()
    for copy in (swap_a, swap_b, back_t, back_u):
        over_tok(copy, "sent")
    for cp in pending:
        cp.wait_send()
    for cp in puts:
        cp.wait()


def sums(v_in, t_in, te, tu, tenant, fill, v_out, t_out, gdown, gup, v_s, t_s, acc, accu, cnt, sem):
    moves = [(v_in, v_s, v_out)]
    for i in range(8):
        rows = pl.ds(i * 32, 32)
        moves.append((t_in.at[rows, :], t_s.at[rows, :], t_out.at[rows, :]))
    loads = [pltpu.make_async_copy(a, b, sem.at[0, i]) for i, (a, b, _) in enumerate(moves)]
    stores = [pltpu.make_async_copy(b, c, sem.at[1, i]) for i, (_, b, c) in enumerate(moves)]
    for cp in loads:
        cp.start()
    f = lax.axis_index("fsdp")
    acc[...] = jnp.zeros_like(acc)
    accu[...] = jnp.zeros_like(accu)

    def clear(i, carry):
        cnt[i] = 0
        return carry

    lax.fori_loop(0, 65, clear, 0)
    lane32 = iota((16, 128), 1) >> 5

    def group(fi):
        def add(b, carry):
            g = tenant[fi * 64 + b] - f * 64
            slot = jnp.where((g >= 0) & (g < 64), g, 64)
            cnt[slot] = cnt[slot] + fill[fi * 64 + b]
            acc[slot] += te[fi, b].astype(F32)
            accu[slot] += jnp.where(lane32 == b // 16, tu[fi, b % 16].astype(F32), 0.0)
            return carry

        lax.fori_loop(0, 64, add, 0)

    group(0)
    for cp, out in zip(loads, stores):
        cp.wait()
        out.start()
    for fi in range(1, 4):
        group(fi)

    def mean(i, carry):
        n = jnp.maximum(cnt[i].astype(F32), 1.0)
        acc[i] = acc[i] / n
        accu[i] = accu[i] / n
        return carry

    lax.fori_loop(0, 64, mean, 0)
    for k in range(8):
        cols = slice(k * 128, (k + 1) * 128)
        gdown[:, cols] = acc[k * 8 : (k + 1) * 8].reshape(128, 256).T
        ut = accu[k * 8 : (k + 1) * 8].reshape(128, 128).T
        gup[:, cols] = ut[0:32] + ut[32:64] + ut[64:96] + ut[96:128]
    for cp in stores:
        cp.wait()


def local(tokens, weight, down, up, cotangent, tenant, fill):
    where = jnp.stack([tenant // 4, tenant % 4])
    any_ = pl.BlockSpec(memory_space=pl.ANY)
    vmem = pl.BlockSpec(memory_space=pltpu.VMEM)
    smem = pl.BlockSpec(memory_space=pltpu.SMEM)
    dma = pltpu.SemaphoreType.DMA
    V = pltpu.VMEM
    v_shape = jax.ShapeDtypeStruct((256, 1024), BF)
    t_shape = jax.ShapeDtypeStruct((256, 8192), BF)
    v, tg, te, tu = pl.pallas_call(
        kernel,
        out_shape=(
            v_shape,
            t_shape,
            jax.ShapeDtypeStruct((4, 1024, 256), BF),
            jax.ShapeDtypeStruct((4, 256, 128), BF),
        ),
        in_specs=[any_, any_, vmem, vmem, vmem, smem, smem, smem],
        out_specs=(vmem, any_, any_, any_),
        scratch_shapes=[
            V((256, 8192), BF),
            V((4, 8192, 256), BF),
            V((4, 256, 256), BF),
            V((4, 256, 256), F32),
            V((256, 8192), F32),
            V((256, 8192), BF),
            V((256, 16, 256), BF),
            V((64, 16, 128), BF),
            V((1024, 256), BF),
            V((1024, 128), BF),
            V((1024, 128), BF),
            V((32, 8192), BF),
            V((32, 32, 128), BF),
            V((32, 1024), BF),
            V((32, 8192), BF),
            V((32, 1024), BF),
            V((1024, 128), BF),
            V((4, 1024, 256), BF),
            V((4, 256, 128), BF),
            V((256, 1024), BF),
            V((256, 32), BF),
            V((256, 32), BF),
            dma((8,)),
            dma((2, 24)),
            dma((2, 12)),
            dma((2, 24)),
            dma((2, 36)),
            dma((2, 48)),
            dma((2, 32)),
            dma((2, 32)),
            dma((2, 32)),
            dma((2, 32)),
        ],
        compiler_params=pltpu.CompilerParams(
            has_side_effects=True, collective_id=1, vmem_limit_bytes=60 * 1024 * 1024
        ),
        cost_estimate=pl.CostEstimate(
            flops=9_000_000_000, bytes_accessed=30_000_000, transcendentals=0
        ),
    )(tokens, weight, down, up, cotangent, tenant, fill, where)
    return pl.pallas_call(
        sums,
        out_shape=(
            v_shape,
            t_shape,
            jax.ShapeDtypeStruct((256, 1024), F32),
            jax.ShapeDtypeStruct((32, 1024), F32),
        ),
        in_specs=[any_, any_, vmem, vmem, smem, smem],
        out_specs=(any_, any_, vmem, vmem),
        scratch_shapes=[
            V((256, 1024), BF),
            V((256, 8192), BF),
            V((65, 16, 256), F32),
            V((65, 16, 128), F32),
            pltpu.SMEM((65,), jnp.int32),
            dma((2, 9)),
        ],
        compiler_params=pltpu.CompilerParams(vmem_limit_bytes=32 * 1024 * 1024),
    )(v, tg, te.reshape(4, 64, 16, 256), tu.reshape(4, 16, 16, 128), tenant, fill)


def solution(mesh):
    placed = (
        P(("fsdp", "tok"), None),
        P(None, "fsdp"),
        P("tok", "fsdp"),
        P("tok", "fsdp"),
        P(("fsdp", "tok"), None),
        P(),
        P(),
    )
    return jax.shard_map(
        local,
        mesh=mesh,
        in_specs=placed,
        out_specs=(
            P(("fsdp", "tok"), None),
            P(("fsdp", "tok"), None),
            P("tok", "fsdp"),
            P("tok", "fsdp"),
        ),
        check_vma=False,
    )
```

time: 289 us -> 123 us (0.43)
  Pallas kernels: 286 us -> 115 us
  local copies, waits for them, and re-layouts: 0 us -> 5.77 us
    pallas_call x2, Pallas kernels: 286 us -> 115 us  [the longest x1 107 us: local(): pl.pallas_call(kernel, out_shape=(v_shape, t_shape, jax.ShapeDtypeStruct(...]
    unnamed x0 -> x12, local copies, waits for them, and re-layouts: none -> 5.77 us
where the time goes in v3:
time: 123 us
  Pallas kernels  115 us (93%)
  local copies, waits for them, and re-layouts  5.77 us (5%)
  other arithmetic  1.28 us (1%)
    pallas_call x1, Pallas kernels, local(): pl.pallas_call(kernel, out_shape=(v_shape, t_shape, jax.ShapeDtypeStruct(...  107 us
    pallas_call x1, Pallas kernels, local(): pl.pallas_call(sums, out_shape=(v_shape, t_shape, jax.ShapeDtypeStruct((2...  7.64 us
    unnamed x12, local copies, waits for them, and re-layouts  5.77 us

profile of v3, /device:TPU:1, one launch (start us, length us, event | category | flops | bytes accessed | tf_op | source)
XLA Modules:
  0.0 122.8 jit_solution(7297805906399320131)
XLA Ops:
  0.6 0.7 and_select_fusion.1
  1.3 0.6 pad_add_fusion.where
  1.9 0.0 copy-start.4
  1.9 0.0 copy-start.5
  1.9 107.5 %shard_map.102 = (bf16[256,1024]{1,0:T(8,128)(2,1)}, bf16[256,8192]{1,0:T(8,128)(2,1)}, bf16[4,1024,256]{2,1,0:T(8,128)(2,1)}, bf16[4,256,128]{2,1,0:T(8,128)(2,1)}) custom-call(bf16[256,8192]{1,0:T(8,128)(2,1)} %x_hbm.1, bf16[8192,256]{1,0:T(8,128)(2,1)} %w_hbm.1, bf16[256,1024]{1,0:T(8,128)(2,1)} %down.1, bf16[32,1024]{1,0:T(8,128)(2,1)} %upmap.1, ...), custom_call_target="tpu_custom_call" | custom-call | flops 8999999488 | bytes 30000000 | tf_op jit(solution)/shard_map/pallas_call | solution.py:588
  109.4 0.0 copy-done.4
  109.4 0.0 copy-done.5
  109.4 0.0 copy-start
  109.4 2.2 %copy-done = bf16[256,8192]{1,0:T(8,128)(2,1)S(1)} copy-done((bf16[256,8192]{1,0:T(8,128)(2,1)S(1)}, bf16[256,8192]{1,0:T(8,128)(2,1)}, u32[]{:S(2)}) %copy-start) | copy-done | bytes 4194328
  111.6 0.0 copy-start.1
  111.6 1.6 %copy-done.1 = bf16[4,1024,256]{2,1,0:T(8,128)(2,1)S(1)} copy-done((bf16[4,1024,256]{2,1,0:T(8,128)(2,1)S(1)}, bf16[4,1024,256]{2,1,0:T(8,128)(2,1)}, u32[]{:S(2)}) %copy-start.1) | copy-done | bytes 2097176
  113.2 0.0 copy-start.2
  113.2 1.0 copy-done.2
  114.2 0.0 copy-start.3
  114.2 0.9 copy-done.3
  115.2 7.6 %shard_map.103 = (bf16[256,1024]{1,0:T(8,128)(2,1)}, bf16[256,8192]{1,0:T(8,128)(2,1)}, f32[256,1024]{1,0:T(8,128)}, f32[32,1024]{1,0:T(8,128)}) custom-call(bf16[256,1024]{1,0:T(8,128)(2,1)S(1)} %copy-done.2, bf16[256,8192]{1,0:T(8,128)(2,1)S(1)} %copy-done, bf16[4,64,16,256]{3,2,1,0:T(8,128)(2,1)S(1)} %bitcast.4, bf16[4,16,16,128]{3,2,1,0:T(8,128)(2,1)S(1)} %bitcast.5, ...), custom_call_target="tpu_custom_call" | custom-call | tf_op jit(solution)/shard_map/pallas_call | solution.py:639
Async XLA Ops:
  1.9 107.5 %copy-start.4 = (s32[256]{0:T(256)S(1)}, s32[256]{0:T(256)}, u32[]{:S(2)}) copy-start(s32[256]{0:T(256)} %tenant.3) | copy-start | bytes 3076
  1.9 107.5 %copy-start.5 = (s32[256]{0:T(256)S(1)}, s32[256]{0:T(256)}, u32[]{:S(2)}) copy-start(s32[256]{0:T(256)} %fill.3) | copy-start | bytes 3076
  109.4 2.2 %copy-start = (bf16[256,8192]{1,0:T(8,128)(2,1)S(1)}, bf16[256,8192]{1,0:T(8,128)(2,1)}, u32[]{:S(2)}) copy-start(bf16[256,8192]{1,0:T(8,128)(2,1)} %get-tuple-element.9.t_in) | copy-start | bytes 12582916
  111.6 1.6 %copy-start.1 = (bf16[4,1024,256]{2,1,0:T(8,128)(2,1)S(1)}, bf16[4,1024,256]{2,1,0:T(8,128)(2,1)}, u32[]{:S(2)}) copy-start(bf16[4,1024,256]{2,1,0:T(8,128)(2,1)} %get-tuple-element.10) | copy-start | bytes 6291460
  113.2 1.0 copy-start.2
  114.2 0.9 copy-start.3

commit v4 on v3

--- a/solution.py
+++ b/solution.py
@@ -34,7 +34,6 @@
     cot,
     tenant,
     fill,
-    where,
     values,
     tgrad,
     te_out,
@@ -61,10 +60,10 @@
     lo,
     ri_s,
     rg_s,
+    quarters,
     loc,
     y_sem,
     wy_sem,
-    wl_sem,
     wx_sem,
     wc_sem,
     pa_sem,
@@ -126,6 +125,13 @@
     get_w = pltpu.make_async_copy(w_hbm, wall.at[f], loc.at[1])
     get_x.start()
     get_w.start()
+
+    def quarter_step(i, carry):
+        for k in range(4):
+            quarters[4 * i + k] = i
+        return carry
+
+    lax.fori_loop(0, 64, quarter_step, 0)
 
     side = jnp.zeros((16, 16, 128), F32)
     for g in range(4):
@@ -186,24 +192,19 @@
     b_start()
 
     base = (x * 1024 + c * 512, 4096 + z * 1024 + c * 512)
-    pos1 = (z, x)
-    dev1 = (dev_z, dev_x)
-    dev2 = (dev_x, dev_z)
-
-    def wslice(fi, row0, n):
-        return wall.at[fi, pl.ds(pl.multiple_of(row0, 64), n), :]
-
-    def sub_at(h, d):
-        return base[h] + up(pos1[h], d) * 128
+    plane = (dev_x, dev_z)
+
+    def wslice(fi, row0):
+        return wall.at[fi, pl.ds(pl.multiple_of(row0, 256), 256), :]
 
     wy = {}
     n_y = 0
     for h in range(2):
         for d, s in ((1, 0), (3, 1), (1, 1), (3, 0)):
-            r0 = sub_at(h, 0) + s * 64
+            r0 = base[h] + s * 256
             cp = remote(
-                w_hbm.at[pl.ds(pl.multiple_of(r0, 64), 64), :],
-                wslice(f, r0, 64),
+                w_hbm.at[pl.ds(pl.multiple_of(r0, 256), 256), :],
+                wslice(f, r0),
                 wy_sem,
                 n_y,
                 dev_y(d),
@@ -212,7 +213,6 @@
             wy[h, d, s] = cp
             pending.append(cp)
             n_y += 1
-    a_start()
 
     b0 = (f * 32 + t) * 2
 
@@ -228,69 +228,52 @@
     va[...] = jnp.zeros_like(va)
     b_near()
 
-    wl = {}
     wx = {}
     wc = {}
     fw = {}
-    counters = {"l": 0, "x": 0, "c": 0}
+    counters = {"x": 0, "c": 0}
     foreign = (up(f, 3), up(f, 1), up(f, 2))
 
-    def same_place(fi, r0, n, sem, kind, dev):
-        cp = remote(wslice(fi, r0, n), wslice(fi, r0, n), sem, counters[kind], dev)
+    def same_place(fi, r0, sem, kind, dev):
+        cp = remote(wslice(fi, r0), wslice(fi, r0), sem, counters[kind], dev)
         counters[kind] += 1
         cp.start()
         pending.append(cp)
         return cp
 
     def to_sibling(fi, r0, key):
-        wc[key] = same_place(fi, r0, 256, wc_sem, "c", sibling)
+        wc[key] = same_place(fi, r0, wc_sem, "c", sibling)
+
+    def to_plane(fi, r0, d, key, h):
+        wx[key] = same_place(fi, r0, wx_sem, "x", plane[h](d))
 
     def w_near(h):
         nonlocal n_y
         for d, s in ((1, 0), (3, 1)):
             wy[h, d, s].wait_recv()
             src = up(f, 4 - d)
-            r0 = sub_at(h, 0) + s * 64
-            cp = remote(wslice(src, r0, 64), wslice(src, r0, 64), wy_sem, n_y, dev_y(d))
+            r0 = base[h] + s * 256
+            cp = remote(wslice(src, r0), wslice(src, r0), wy_sem, n_y, dev_y(d))
             n_y += 1
             cp.start()
             fw[h, s] = cp
             pending.append(cp)
-        for d, s in ((1, 1), (3, 0)):
-            wy[h, d, s].wait_recv()
-        for fi in range(2):
-            for dd in (1, 3):
-                wl[h, dd, fi] = same_place(
-                    foreign[fi], sub_at(h, 0), 128, wl_sem, "l", dev1[h](dd)
-                )
+        for d, s in ((1, 0), (3, 1), (1, 1), (3, 0)):
+            if (d, s) in ((1, 1), (3, 0)):
+                wy[h, d, s].wait_recv()
+            fi = 0 if d == 1 else 1
+            r0 = base[h] + s * 256
+            for dd in (1, 3) if s == 0 else (3, 1):
+                to_plane(foreign[fi], r0, dd, (h, dd, fi, s), h)
+            to_sibling(foreign[fi], r0, (h, 0, fi, s))
 
     def w_far(h):
         for s in range(2):
             fw[h, s].wait_recv()
-        for dd in (1, 3):
-            wl[h, dd, 2] = same_place(
-                foreign[2], sub_at(h, 0), 128, wl_sem, "l", dev1[h](dd)
-            )
-
-    def w_line(h, fi):
-        for d, s in ((1, 0), (3, 1)):
-            wl[h, d, fi].wait_recv()
-            wl[h, 2, fi, s] = same_place(
-                foreign[fi], sub_at(h, 4 - d) + s * 64, 64, wl_sem, "l", dev1[h](d)
-            )
-
-    def to_plane(fi, r0, d, key, h):
-        wx[key] = same_place(fi, r0, 256, wx_sem, "x", dev2[h](d))
-
-    def w_plane(h, fi):
-        for s in range(2):
-            wl[h, 2, fi, s].wait_recv()
-        for s in range(2):
             r0 = base[h] + s * 256
             for dd in (1, 3) if s == 0 else (3, 1):
-                to_plane(foreign[fi], r0, dd, (h, dd, fi, s), h)
-        for s in range(2):
-            to_sibling(foreign[fi], base[h] + s * 256, (h, 0, fi, s))
+                to_plane(foreign[2], r0, dd, (h, dd, 2, s), h)
+            to_sibling(foreign[2], r0, (h, 0, 2, s))
 
     def here(h, d):
         if h == 0:
@@ -308,6 +291,11 @@
             r0 = here(h, 4 - d) + s * 256
             to_sibling(foreign[fi], r0, (h, d, fi, s))
 
+    def w_end(h, fi):
+        for s in range(2):
+            wx[h, 2, fi, s].wait_recv()
+            to_sibling(foreign[fi], here(h, 2) + s * 256, (h, 2, fi, s))
+
     b_far()
 
     lane32 = iota((16, 128), 1) >> 5
@@ -315,9 +303,10 @@
     ej = iota((128, 128), 1)
 
     def pick_b(b, carry):
-        v = ab_b[where[0, f * 64 + b]]
+        quarter = quarters[tenant[f * 64 + b]]
+        v = ab_b[quarter]
         vb[my_cols(b, 16), :] = jnp.where(
-            lane32 == where[1, f * 64 + b], v.astype(F32), 0.0
+            lane32 == tenant[f * 64 + b] - 4 * quarter, v.astype(F32), 0.0
         ).astype(BF)
         return carry
 
@@ -368,7 +357,6 @@
 
     get_x.wait()
     w_near(0)
-    w_near(1)
 
     over_tok(swap_b, "recv")
     for q in range(8):
@@ -391,12 +379,8 @@
     over_tok(back_t, "start")
     te[f, my_cols(t, 32), :] = gs[:, my_cols(t, 256)]
 
-    w_far(0)
-    w_far(1)
-    for h in range(2):
-        w_line(h, 0)
-        w_line(h, 1)
-    a_forward()
+    w_near(1)
+    a_start()
     get_w.wait()
 
     def own_step(k, carry):
@@ -408,25 +392,24 @@
 
     lax.fori_loop(0, 8, own_step, 0)
     for h in range(2):
-        w_line(h, 2)
-    for fi in range(2):
-        for h in range(2):
-            w_plane(h, fi)
+        w_far(h)
     over_tok(back_t, "recv")
-    t_start()
     put_own = pltpu.make_async_copy(te.at[f], te_out.at[f], loc.at[3])
     put_own.start()
-    for h in range(2):
-        w_plane(h, 2)
+    w_along(0, 0)
+    a_forward()
+    w_along(1, 0)
     a_near()
+    t_start()
+    lax.fori_loop(8, 20, own_step, 0)
     a_far()
     lax.fori_loop(0, 64, pick_a, 0)
     over_tok(swap_a, "start")
     at[:, my_cols(t, 256)] = send_a[my_cols(t, 32), :]
-    for h in range(2):
-        w_along(h, 0)
-    lax.fori_loop(8, 32, own_step, 0)
+    w_along(0, 1)
+    w_along(1, 1)
     t_forward()
+    lax.fori_loop(20, 32, own_step, 0)
 
     over_tok(swap_a, "recv")
 
@@ -439,23 +422,14 @@
     for j in range(4):
         us[:, j * 256 : (j + 1) * 256] = (SCALE * mm(ri_s[...], go[j], TN)).astype(BF)
     over_tok(back_u, "start")
+    w_end(0, 0)
+    w_end(1, 0)
     ur[my_cols(t, 32), :] = us[:, my_cols(t // 4, 128)]
 
-    for h in range(2):
-        w_along(h, 1)
     for j in range(4):
         lo[:, j * 256 : (j + 1) * 256] = (
             SCALE * mm(ri_s[...], bt[:, j * 256 : (j + 1) * 256])
         ).astype(BF)
-
-    over_tok(back_u, "recv")
-    packed = jnp.zeros((256, 128), F32)
-    for q in range(4):
-        e = pick(((el >> 5) == (t & 3)) & ((ej >> 5) == q) & ((el & 31) == (ej & 31)))
-        packed = packed + mm(ur[q * 256 : (q + 1) * 256, :], e)
-    tu[f] = packed.astype(BF)
-    u_start()
-
     def tile(row0):
         cols = pl.ds(pl.multiple_of(row0, 256), 256)
         xk = xv[:, cols]
@@ -482,18 +456,29 @@
                 for s in range(2):
                     wc[h, d, fi, s].wait_recv()
 
-    for h in range(2):
-        w_along(h, 2)
+    over_tok(back_u, "recv")
+    packed = jnp.zeros((256, 128), F32)
+    for q in range(4):
+        e = pick(((el >> 5) == (t & 3)) & ((ej >> 5) == q) & ((el & 31) == (ej & 31)))
+        packed = packed + mm(ur[q * 256 : (q + 1) * 256, :], e)
+    tu[f] = packed.astype(BF)
+    u_start()
+    w_along(0, 2)
+    w_along(1, 2)
     await_sibling(0)
     tiles(0)
+    w_end(0, 1)
+    w_end(1, 1)
     u_forward()
-    for fi in range(3):
-        for h in range(2):
-            for s in range(2):
-                wx[h, 2, fi, s].wait_recv()
-                to_sibling(foreign[fi], here(h, 2) + s * 256, (h, 2, fi, s))
     await_sibling(1)
     tiles(3)
+    t_near()
+    puts = [put_own]
+    for i, fi in enumerate(foreign[:2]):
+        puts.append(pltpu.make_async_copy(te.at[fi], te_out.at[fi], loc.at[4 + i]))
+        puts[-1].start()
+    w_end(0, 2)
+    w_end(1, 2)
     await_sibling(3)
     tiles(1)
     await_sibling(2)
@@ -502,12 +487,9 @@
     for j in range(4):
         cols = slice(j * 256, (j + 1) * 256)
         values[:, cols] = jnp.where(used, va[j] + lo[:, cols].astype(F32), 0.0).astype(BF)
-    t_near()
     t_far()
-    puts = [put_own]
-    for i, fi in enumerate(foreign):
-        puts.append(pltpu.make_async_copy(te.at[fi], te_out.at[fi], loc.at[4 + i]))
-        puts[-1].start()
+    puts.append(pltpu.make_async_copy(te.at[foreign[2]], te_out.at[foreign[2]], loc.at[6]))
+    puts[-1].start()
     u_near()
     u_far()
     puts.append(pltpu.make_async_copy(tu, tu_out, loc.at[7]))
@@ -522,14 +504,19 @@
         cp.wait()
 
 
-def sums(v_in, t_in, te, tu, tenant, fill, v_out, t_out, gdown, gup, v_s, t_s, acc, accu, cnt, sem):
+def sums(v_in, t_in, te_in, tu_in, tenant, fill, v_out, t_out, gdown, gup, *scratch):
+    v_s, t_s, te, tu, acc, accu, cnt, mine, sem = scratch
+    first = [
+        pltpu.make_async_copy(te_in, te, sem.at[0, 9]),
+        pltpu.make_async_copy(tu_in, tu, sem.at[0, 10]),
+    ]
     moves = [(v_in, v_s, v_out)]
     for i in range(8):
         rows = pl.ds(i * 32, 32)
         moves.append((t_in.at[rows, :], t_s.at[rows, :], t_out.at[rows, :]))
     loads = [pltpu.make_async_copy(a, b, sem.at[0, i]) for i, (a, b, _) in enumerate(moves)]
     stores = [pltpu.make_async_copy(b, c, sem.at[1, i]) for i, (_, b, c) in enumerate(moves)]
-    for cp in loads:
+    for cp in first + loads:
         cp.start()
     f = lax.axis_index("fsdp")
     acc[...] = jnp.zeros_like(acc)
@@ -540,25 +527,33 @@
         return carry
 
     lax.fori_loop(0, 65, clear, 0)
+
+    def note(b, n):
+        g = tenant[b] - f * 64
+        own = (g >= 0) & (g < 64)
+        slot = jnp.where(own, g, 64)
+        cnt[slot] = cnt[slot] + fill[b]
+        mine[n] = b
+        return n + jnp.where(own, 1, 0)
+
+    count = lax.fori_loop(0, 256, note, 0)
     lane32 = iota((16, 128), 1) >> 5
-
-    def group(fi):
-        def add(b, carry):
-            g = tenant[fi * 64 + b] - f * 64
-            slot = jnp.where((g >= 0) & (g < 64), g, 64)
-            cnt[slot] = cnt[slot] + fill[fi * 64 + b]
-            acc[slot] += te[fi, b].astype(F32)
-            accu[slot] += jnp.where(lane32 == b // 16, tu[fi, b % 16].astype(F32), 0.0)
-            return carry
-
-        lax.fori_loop(0, 64, add, 0)
-
-    group(0)
+    for cp in first:
+        cp.wait()
     for cp, out in zip(loads, stores):
         cp.wait()
         out.start()
-    for fi in range(1, 4):
-        group(fi)
+
+    def add(i, carry):
+        b = mine[i]
+        slot = tenant[b] - f * 64
+        fi = b // 64
+        k = b % 64
+        acc[slot] += te[fi, k].astype(F32)
+        accu[slot] += jnp.where(lane32 == k // 16, tu[fi, k % 16].astype(F32), 0.0)
+        return carry
+
+    lax.fori_loop(0, count, add, 0)
 
     def mean(i, carry):
         n = jnp.maximum(cnt[i].astype(F32), 1.0)
@@ -566,7 +561,7 @@
         accu[i] = accu[i] / n
         return carry
 
-    lax.fori_loop(0, 64, mean, 0)
+    lax.fori_loop(0, 64, mean, 0, unroll=4)
     for k in range(8):
         cols = slice(k * 128, (k + 1) * 128)
         gdown[:, cols] = acc[k * 8 : (k + 1) * 8].reshape(128, 256).T
@@ -577,7 +572,6 @@
 
 
 def local(tokens, weight, down, up, cotangent, tenant, fill):
-    where = jnp.stack([tenant // 4, tenant % 4])
     any_ = pl.BlockSpec(memory_space=pl.ANY)
     vmem = pl.BlockSpec(memory_space=pltpu.VMEM)
     smem = pl.BlockSpec(memory_space=pltpu.SMEM)
@@ -593,7 +587,7 @@
             jax.ShapeDtypeStruct((4, 1024, 256), BF),
             jax.ShapeDtypeStruct((4, 256, 128), BF),
         ),
-        in_specs=[any_, any_, vmem, vmem, vmem, smem, smem, smem],
+        in_specs=[any_, any_, vmem, vmem, vmem, smem, smem],
         out_specs=(vmem, any_, any_, any_),
         scratch_shapes=[
             V((256, 8192), BF),
@@ -618,10 +612,10 @@
             V((256, 1024), BF),
             V((256, 32), BF),
             V((256, 32), BF),
+            pltpu.SMEM((256,), jnp.int32),
             dma((8,)),
             dma((2, 24)),
             dma((2, 12)),
-            dma((2, 24)),
             dma((2, 36)),
             dma((2, 48)),
             dma((2, 32)),
@@ -635,7 +629,7 @@
         cost_estimate=pl.CostEstimate(
             flops=9_000_000_000, bytes_accessed=30_000_000, transcendentals=0
         ),
-    )(tokens, weight, down, up, cotangent, tenant, fill, where)
+    )(tokens, weight, down, up, cotangent, tenant, fill)
     return pl.pallas_call(
         sums,
         out_shape=(
@@ -644,17 +638,20 @@
             jax.ShapeDtypeStruct((256, 1024), F32),
             jax.ShapeDtypeStruct((32, 1024), F32),
         ),
-        in_specs=[any_, any_, vmem, vmem, smem, smem],
+        in_specs=[any_, any_, any_, any_, smem, smem],
         out_specs=(any_, any_, vmem, vmem),
         scratch_shapes=[
             V((256, 1024), BF),
             V((256, 8192), BF),
+            V((4, 64, 16, 256), BF),
+            V((4, 16, 16, 128), BF),
             V((65, 16, 256), F32),
             V((65, 16, 128), F32),
             pltpu.SMEM((65,), jnp.int32),
-            dma((2, 9)),
+            pltpu.SMEM((256,), jnp.int32),
+            dma((2, 11)),
         ],
-        compiler_params=pltpu.CompilerParams(vmem_limit_bytes=32 * 1024 * 1024),
+        compiler_params=pltpu.CompilerParams(vmem_limit_bytes=60 * 1024 * 1024),
     )(v, tg, te.reshape(4, 64, 16, 256), tu.reshape(4, 16, 16, 128), tenant, fill)
 
 

time: 123 us -> 108 us (0.88)
  Pallas kernels: 115 us -> 107 us
  local copies, waits for them, and re-layouts: 5.77 us -> 0 us
  other arithmetic: 1.28 us -> 0 us
    pallas_call x1, Pallas kernels: 107 us -> 99.8 us  [local(): pl.pallas_call(kernel, out_shape=(v_shape, t_shape, jax.ShapeDtypeStruct(...]
    unnamed x12 -> x0, local copies, waits for them, and re-layouts: 5.77 us -> none
where the time goes in v4:
time: 108 us
  Pallas kernels  107 us (99%)
    pallas_call x1, Pallas kernels, local(): pl.pallas_call(kernel, out_shape=(v_shape, t_shape, jax.ShapeDtypeStruct(...  99.8 us
    pallas_call x1, Pallas kernels, local(): pl.pallas_call(sums, out_shape=(v_shape, t_shape, jax.ShapeDtypeStruct((2...  7.42 us

profile of v4, /device:TPU:1, one launch (start us, length us, event | category | flops | bytes accessed | tf_op | source)
XLA Modules:
  0.0 107.9 jit_solution(3988508339035342944)
XLA Ops:
  0.6 99.8 %shard_map.102 = (bf16[256,1024]{1,0:T(8,128)(2,1)}, bf16[256,8192]{1,0:T(8,128)(2,1)}, bf16[4,1024,256]{2,1,0:T(8,128)(2,1)}, bf16[4,256,128]{2,1,0:T(8,128)(2,1)}) custom-call(bf16[256,8192]{1,0:T(8,128)(2,1)} %x_hbm.1, bf16[8192,256]{1,0:T(8,128)(2,1)} %w_hbm.1, bf16[256,1024]{1,0:T(8,128)(2,1)} %down.1, bf16[32,1024]{1,0:T(8,128)(2,1)} %upmap.1, ...), custom_call_target="tpu_custom_call" | custom-call | flops 8999999488 | bytes 30000000 | tf_op jit(solution)/shard_map/pallas_call | solution.py:582
  100.5 7.4 %shard_map.103 = (bf16[256,1024]{1,0:T(8,128)(2,1)}, bf16[256,8192]{1,0:T(8,128)(2,1)}, f32[256,1024]{1,0:T(8,128)}, f32[32,1024]{1,0:T(8,128)}) custom-call(bf16[256,1024]{1,0:T(8,128)(2,1)} %get-tuple-element.8.v_in, bf16[256,8192]{1,0:T(8,128)(2,1)} %get-tuple-element.9.t_in, bf16[4,64,16,256]{3,2,1,0:T(8,128)(2,1)} %bitcast.2, ...), custom_call_target="tpu_custom_call" | custom-call | tf_op jit(solution)/shard_map/pallas_call | solution.py:633

commit v5 on v4

--- a/solution.py
+++ b/solution.py
@@ -54,6 +54,7 @@
     bt,
     gs,
     us,
+    usj,
     ur,
     te,
     tu,
@@ -139,7 +140,6 @@
         moved = mm(upmap[...], place, TN).reshape(16, 64, 128)
         side = side + moved[:, g * 16 : (g + 1) * 16, :]
     ab_b[pl.ds(f * 16, 16)] = side.astype(BF)
-    ab_a[pl.ds(f * 64, 64)] = down[...].astype(F32).T.astype(BF).reshape(64, 16, 256)
 
     pl.semaphore_wait(barrier, 33)
 
@@ -199,7 +199,9 @@
 
     wy = {}
     n_y = 0
-    for h in range(2):
+
+    def wy_start(h):
+        nonlocal n_y
         for d, s in ((1, 0), (3, 1), (1, 1), (3, 0)):
             r0 = base[h] + s * 256
             cp = remote(
@@ -213,6 +215,9 @@
             wy[h, d, s] = cp
             pending.append(cp)
             n_y += 1
+
+    wy_start(0)
+    ab_a[pl.ds(f * 64, 64)] = down[...].astype(F32).T.astype(BF).reshape(64, 16, 256)
 
     b0 = (f * 32 + t) * 2
 
@@ -302,13 +307,18 @@
     el = iota((128, 128), 0)
     ej = iota((128, 128), 1)
 
-    def pick_b(b, carry):
-        quarter = quarters[tenant[f * 64 + b]]
-        v = ab_b[quarter]
-        vb[my_cols(b, 16), :] = jnp.where(
-            lane32 == tenant[f * 64 + b] - 4 * quarter, v.astype(F32), 0.0
-        ).astype(BF)
-        return carry
+    def pick_b(i, carry):
+        for j in range(2):
+            g = tenant[f * 64 + 2 * i + j]
+            quarter = quarters[g]
+            v = ab_b[quarter]
+            vb[j, my_cols(i, 16), :] = jnp.where(
+                lane32 == g - 4 * quarter, v.astype(F32), 0.0
+            ).astype(BF)
+        return carry
+
+    def lanes(i, j):
+        return pick((el == i * 32 + (ej & 31)) & ((ej >> 5) == j))
 
     def pick_a(b, carry):
         send_a[my_cols(b, 16), :] = ab_a[tenant[f * 64 + b]]
@@ -322,7 +332,7 @@
 
     def swap_b(d):
         to = lax.rem(t + d, 32)
-        return remote(send_b.at[my_cols(to, 32), :], recv_b.at[t], pb_sem, d, (f, to))
+        return remote(send_b.at[to], recv_b.at[t // 4, t % 4], pb_sem, d, (f, to))
 
     def back_t(d):
         to = lax.rem(t + d, 32)
@@ -333,7 +343,7 @@
     def back_u(d):
         to = lax.rem(t + d, 32)
         return remote(
-            us.at[:, my_cols(to // 4, 128)], ur.at[my_cols(t, 32), :], gu_sem, d, (f, to)
+            us.at[to // 4, to % 4], ur.at[t // 4, t % 4], gu_sem, d, (f, to)
         )
 
     def over_tok(copy, act):
@@ -349,21 +359,28 @@
 
         lax.fori_loop(1, 32, step, 0)
 
-    lax.fori_loop(0, 64, pick_b, 0)
-    spread = pick(((el & 31) == (ej & 31)) & ((ej >> 5) == (t & 3)))
-    send_b[...] = mm(vb[...], spread).astype(BF)
+    lax.fori_loop(0, 32, pick_b, 0)
+    for j in range(2):
+        spread = pick(((el & 31) == (ej & 31)) & ((ej >> 5) == j))
+        moved = mm(vb[j], spread)
+        side = moved if j == 0 else side + moved
+    send_b[...] = side.astype(BF).reshape(32, 16, 128)
     over_tok(swap_b, "start")
-    recv_b[t] = send_b[my_cols(t, 32), :]
-
+    recv_b[t // 4, t % 4] = send_b[t]
+
+    wy_start(1)
     get_x.wait()
     w_near(0)
 
     over_tok(swap_b, "recv")
-    for q in range(8):
-        total = recv_b[4 * q]
-        for i in range(1, 4):
-            total = total + recv_b[4 * q + i]
-        bt[:, q * 128 : (q + 1) * 128] = total
+    for j in range(2):
+        total = jnp.zeros((128, 128), F32)
+        for i in range(4):
+            total = total + mm(recv_b[:, i].reshape(128, 128), lanes(j, i))
+        for q in range(8):
+            bt[j * 16 : (j + 1) * 16, q * 128 : (q + 1) * 128] = total[
+                q * 16 : (q + 1) * 16, :
+            ].astype(BF)
     diagonal = (iota((256, 32), 0) >> 7) == (iota((256, 32), 1) >> 4)
     rank_grad = jnp.zeros((256, 32), F32)
     for j in range(4):
@@ -419,12 +436,20 @@
 
     rank_in = lax.fori_loop(0, 8, rank_step, jnp.zeros((256, 32), F32))
     ri_s[...] = jnp.where(diagonal, rank_in, 0.0).astype(BF)
-    for j in range(4):
-        us[:, j * 256 : (j + 1) * 256] = (SCALE * mm(ri_s[...], go[j], TN)).astype(BF)
+    for k in range(4):
+        part = (SCALE * mm(ri_s[...], go[k], TN)).astype(BF)
+        for q in range(2):
+            for j in range(2):
+                usj[j, (2 * k + q) * 16 : (2 * k + q + 1) * 16, :] = part[
+                    j * 16 : (j + 1) * 16, q * 128 : (q + 1) * 128
+                ]
+    for i in range(4):
+        part = mm(usj[0], lanes(i, 0)) + mm(usj[1], lanes(i, 1))
+        us[:, i] = part.astype(BF).reshape(8, 16, 128)
     over_tok(back_u, "start")
     w_end(0, 0)
     w_end(1, 0)
-    ur[my_cols(t, 32), :] = us[:, my_cols(t // 4, 128)]
+    ur[t // 4, t % 4] = us[t // 4, t % 4]
 
     for j in range(4):
         lo[:, j * 256 : (j + 1) * 256] = (
@@ -457,11 +482,11 @@
                     wc[h, d, fi, s].wait_recv()
 
     over_tok(back_u, "recv")
-    packed = jnp.zeros((256, 128), F32)
-    for q in range(4):
-        e = pick(((el >> 5) == (t & 3)) & ((ej >> 5) == q) & ((el & 31) == (ej & 31)))
-        packed = packed + mm(ur[q * 256 : (q + 1) * 256, :], e)
-    tu[f] = packed.astype(BF)
+    for j in range(2):
+        packed = jnp.zeros((128, 128), F32)
+        for q in range(4):
+            packed = packed + mm(ur[2 * q : 2 * q + 2].reshape(128, 128), lanes(j, q))
+        tu[f, j * 128 : (j + 1) * 128, :] = packed.astype(BF)
     u_start()
     w_along(0, 2)
     w_along(1, 2)
@@ -550,7 +575,7 @@
         fi = b // 64
         k = b % 64
         acc[slot] += te[fi, k].astype(F32)
-        accu[slot] += jnp.where(lane32 == k // 16, tu[fi, k % 16].astype(F32), 0.0)
+        accu[slot] += jnp.where(lane32 == k // 16, tu[fi, (k % 2) * 8 + (k % 16) // 2].astype(F32), 0.0)
         return carry
 
     lax.fori_loop(0, count, add, 0)
@@ -599,14 +624,15 @@
             V((256, 16, 256), BF),
             V((64, 16, 128), BF),
             V((1024, 256), BF),
-            V((1024, 128), BF),
-            V((1024, 128), BF),
+            V((2, 512, 128), BF),
+            V((32, 16, 128), BF),
             V((32, 8192), BF),
-            V((32, 32, 128), BF),
+            V((8, 4, 16, 128), BF),
             V((32, 1024), BF),
             V((32, 8192), BF),
-            V((32, 1024), BF),
-            V((1024, 128), BF),
+            V((8, 4, 16, 128), BF),
+            V((2, 128, 128), BF),
+            V((8, 4, 16, 128), BF),
             V((4, 1024, 256), BF),
             V((4, 256, 128), BF),
             V((256, 1024), BF),

time: 108 us -> 101 us (0.935)
  Pallas kernels: 107 us -> 99.8 us
    pallas_call x1, Pallas kernels: 99.8 us -> 92 us  [local(): pl.pallas_call(kernel, out_shape=(v_shape, t_shape, jax.ShapeDtypeStruct(...]
where the time goes in v5:
time: 101 us; the launch traced here: 100 us
  Pallas kernels  99.8 us (99%)
    pallas_call x1, Pallas kernels, local(): pl.pallas_call(kernel, out_shape=(v_shape, t_shape, jax.ShapeDtypeStruct(...  92 us
    pallas_call x1, Pallas kernels, local(): pl.pallas_call(sums, out_shape=(v_shape, t_shape, jax.ShapeDtypeStruct((2...  7.83 us

profile of v5, /device:TPU:1, one launch (start us, length us, event | category | flops | bytes accessed | tf_op | source)
XLA Modules:
  0.0 100.4 jit_solution(18323507290607191123)
XLA Ops:
  0.6 92.0 %shard_map.102 = (bf16[256,1024]{1,0:T(8,128)(2,1)}, bf16[256,8192]{1,0:T(8,128)(2,1)}, bf16[4,1024,256]{2,1,0:T(8,128)(2,1)}, bf16[4,256,128]{2,1,0:T(8,128)(2,1)}) custom-call(bf16[256,8192]{1,0:T(8,128)(2,1)} %x_hbm.1, bf16[8192,256]{1,0:T(8,128)(2,1)} %w_hbm.1, bf16[256,1024]{1,0:T(8,128)(2,1)} %down.1, bf16[32,1024]{1,0:T(8,128)(2,1)} %upmap.1, ...), custom_call_target="tpu_custom_call" | custom-call | flops 8999999488 | bytes 30000000 | tf_op jit(solution)/shard_map/pallas_call | solution.py:607
  92.6 7.8 %shard_map.103 = (bf16[256,1024]{1,0:T(8,128)(2,1)}, bf16[256,8192]{1,0:T(8,128)(2,1)}, f32[256,1024]{1,0:T(8,128)}, f32[32,1024]{1,0:T(8,128)}) custom-call(bf16[256,1024]{1,0:T(8,128)(2,1)} %get-tuple-element.8.v_in, bf16[256,8192]{1,0:T(8,128)(2,1)} %get-tuple-element.9.t_in, bf16[4,64,16,256]{3,2,1,0:T(8,128)(2,1)} %bitcast.2, ...), custom_call_target="tpu_custom_call" | custom-call | tf_op jit(solution)/shard_map/pallas_call | solution.py:659

commit v6 on v5

--- a/solution.py
+++ b/solution.py
@@ -425,6 +425,7 @@
     at[:, my_cols(t, 256)] = send_a[my_cols(t, 32), :]
     w_along(0, 1)
     w_along(1, 1)
+    early = len(pending)
     t_forward()
     lax.fori_loop(20, 32, own_step, 0)
 
@@ -455,29 +456,34 @@
         lo[:, j * 256 : (j + 1) * 256] = (
             SCALE * mm(ri_s[...], bt[:, j * 256 : (j + 1) * 256])
         ).astype(BF)
-    def tile(row0):
+    def tile(row0, shards, last):
         cols = pl.ds(pl.multiple_of(row0, 256), 256)
         xk = xv[:, cols]
-        total = tga[:, cols] + mm(rg_s[...], at[:, cols])
-        for fi in foreign:
+        total = tga[:, cols]
+        if last:
+            total = total + mm(rg_s[...], at[:, cols])
+        for fi in shards:
             wk = wall[fi, cols, :]
             va[fi] += mm(xk, wk)
             total = total + mm(go[fi], wk, NT)
+        if not last:
+            tga[:, cols] = total
+            return
         tg_v[:, cols] = total.astype(BF)
         pltpu.make_async_copy(tg_v.at[:, cols], tgrad.at[:, cols], loc.at[2]).start()
 
-    def tiles(d):
+    def tiles(d, shards=foreign, last=True):
         def step(i, carry):
             h = i // 4
             pos = jnp.where(h == 0, lax.rem(x + d, 4), lax.rem(z + d, 4))
-            tile(h * 4096 + pos * 1024 + (i % 4) * 256)
+            tile(h * 4096 + pos * 1024 + (i % 4) * 256, shards, last)
             return carry
 
         lax.fori_loop(0, 8, step, 0)
 
-    def await_sibling(d):
+    def await_sibling(d, shards=range(3)):
         for h in range(2):
-            for fi in range(3):
+            for fi in shards:
                 for s in range(2):
                     wc[h, d, fi, s].wait_recv()
 
@@ -506,8 +512,14 @@
     w_end(1, 2)
     await_sibling(3)
     tiles(1)
-    await_sibling(2)
-    tiles(2)
+    await_sibling(2, (0, 1))
+    tiles(2, foreign[:2], False)
+    for copy in (swap_a, swap_b, back_t, back_u):
+        over_tok(copy, "sent")
+    for cp in pending[:early]:
+        cp.wait_send()
+    await_sibling(2, (2,))
+    tiles(2, foreign[2:])
     used = used_rows()
     for j in range(4):
         cols = slice(j * 256, (j + 1) * 256)
@@ -521,9 +533,7 @@
     puts[-1].start()
 
     pltpu.make_async_copy(tg_v, tgrad, loc.at[2]).wait()
-    for copy in (swap_a, swap_b, back_t, back_u):
-        over_tok(copy, "sent")
-    for cp in pending:
+    for cp in pending[early:]:
         cp.wait_send()
     for cp in puts:
         cp.wait()

time: 101 us -> 102 us (level)
  Pallas kernels: 99.8 us -> 101 us
    pallas_call x1, Pallas kernels: 92 us -> 93.8 us  [local(): pl.pallas_call(kernel, out_shape=(v_shape, t_shape, jax.ShapeDtypeStruct(...]
where the time goes in v6:
time: 102 us
  Pallas kernels  101 us (99%)
    pallas_call x1, Pallas kernels, local(): pl.pallas_call(kernel, out_shape=(v_shape, t_shape, jax.ShapeDtypeStruct(...  93.8 us
    pallas_call x1, Pallas kernels, local(): pl.pallas_call(sums, out_shape=(v_shape, t_shape, jax.ShapeDtypeStruct((2...  7.66 us

profile of v6, /device:TPU:1, one launch (start us, length us, event | category | flops | bytes accessed | tf_op | source)
XLA Modules:
  0.0 102.1 jit_solution(4250599243058185062)
XLA Ops:
  0.6 93.8 %shard_map.102 = (bf16[256,1024]{1,0:T(8,128)(2,1)}, bf16[256,8192]{1,0:T(8,128)(2,1)}, bf16[4,1024,256]{2,1,0:T(8,128)(2,1)}, bf16[4,256,128]{2,1,0:T(8,128)(2,1)}) custom-call(bf16[256,8192]{1,0:T(8,128)(2,1)} %x_hbm.1, bf16[8192,256]{1,0:T(8,128)(2,1)} %w_hbm.1, bf16[256,1024]{1,0:T(8,128)(2,1)} %down.1, bf16[32,1024]{1,0:T(8,128)(2,1)} %upmap.1, ...), custom_call_target="tpu_custom_call" | custom-call | flops 8999999488 | bytes 30000000 | tf_op jit(solution)/shard_map/pallas_call | solution.py:617
  94.5 7.7 %shard_map.103 = (bf16[256,1024]{1,0:T(8,128)(2,1)}, bf16[256,8192]{1,0:T(8,128)(2,1)}, f32[256,1024]{1,0:T(8,128)}, f32[32,1024]{1,0:T(8,128)}) custom-call(bf16[256,1024]{1,0:T(8,128)(2,1)} %get-tuple-element.8.v_in, bf16[256,8192]{1,0:T(8,128)(2,1)} %get-tuple-element.9.t_in, bf16[4,64,16,256]{3,2,1,0:T(8,128)(2,1)} %bitcast.2, ...), custom_call_target="tpu_custom_call" | custom-call | tf_op jit(solution)/shard_map/pallas_call | solution.py:669

commit v7 on v5

--- a/solution.py
+++ b/solution.py
@@ -565,9 +565,6 @@
     lane32 = iota((16, 128), 1) >> 5
     for cp in first:
         cp.wait()
-    for cp, out in zip(loads, stores):
-        cp.wait()
-        out.start()
 
     def add(i, carry):
         b = mine[i]
@@ -578,7 +575,11 @@
         accu[slot] += jnp.where(lane32 == k // 16, tu[fi, (k % 2) * 8 + (k % 16) // 2].astype(F32), 0.0)
         return carry
 
-    lax.fori_loop(0, count, add, 0)
+    lax.fori_loop(0, count // 2, add, 0)
+    for cp, out in zip(loads, stores):
+        cp.wait()
+        out.start()
+    lax.fori_loop(count // 2, count, add, 0)
 
     def mean(i, carry):
         n = jnp.maximum(cnt[i].astype(F32), 1.0)

time: 101 us -> 101 us (level)
  no operation moved by 1% of the time
where the time goes in v7:
time: 101 us
  Pallas kernels  100 us (99%)
    pallas_call x1, Pallas kernels, local(): pl.pallas_call(kernel, out_shape=(v_shape, t_shape, jax.ShapeDtypeStruct(...  92 us
    pallas_call x1, Pallas kernels, local(): pl.pallas_call(sums, out_shape=(v_shape, t_shape, jax.ShapeDtypeStruct((2...  8.46 us

profile of v7, /device:TPU:1, one launch (start us, length us, event | category | flops | bytes accessed | tf_op | source)
XLA Modules:
  0.0 101.1 jit_solution(10067350874156488335)
XLA Ops:
  0.6 92.0 %shard_map.102 = (bf16[256,1024]{1,0:T(8,128)(2,1)}, bf16[256,8192]{1,0:T(8,128)(2,1)}, bf16[4,1024,256]{2,1,0:T(8,128)(2,1)}, bf16[4,256,128]{2,1,0:T(8,128)(2,1)}) custom-call(bf16[256,8192]{1,0:T(8,128)(2,1)} %x_hbm.1, bf16[8192,256]{1,0:T(8,128)(2,1)} %w_hbm.1, bf16[256,1024]{1,0:T(8,128)(2,1)} %down.1, bf16[32,1024]{1,0:T(8,128)(2,1)} %upmap.1, ...), custom_call_target="tpu_custom_call" | custom-call | flops 8999999488 | bytes 30000000 | tf_op jit(solution)/shard_map/pallas_call | solution.py:608
  92.6 8.5 %shard_map.103 = (bf16[256,1024]{1,0:T(8,128)(2,1)}, bf16[256,8192]{1,0:T(8,128)(2,1)}, f32[256,1024]{1,0:T(8,128)}, f32[32,1024]{1,0:T(8,128)}) custom-call(bf16[256,1024]{1,0:T(8,128)(2,1)} %get-tuple-element.8.v_in, bf16[256,8192]{1,0:T(8,128)(2,1)} %get-tuple-element.9.t_in, bf16[4,64,16,256]{3,2,1,0:T(8,128)(2,1)} %bitcast.2, ...), custom_call_target="tpu_custom_call" | custom-call | tf_op jit(solution)/shard_map/pallas_call | solution.py:660
